TPU v7x, 512 devices: a whole 4x4x16 slice. The times are simulated.
512 devices in a mesh: dp: 64 (over x_lo, z, core), tensor: 8 (over x_hi, y).
Axes of the slice: x: 4 (x_hi: 2, x_lo: 2; x = x_hi * 2 + x_lo), y: 4, z: 16, core: 2. Of those that a mesh axis runs over, the one named last changes fastest.
Arguments:
- tokens: bfloat16 [16384, 8192], P('dp', 'tensor'), may hold values from -6 to 6
- cotangent: bfloat16 [16384, 8192], P('dp', 'tensor'), may hold values from -6 to 6
- gate_inner: bfloat16 [64, 128, 128], P('tensor', 'dp'), may hold values from -0.5 to 0.5
- gate_outer: bfloat16 [64, 128, 128], P('tensor', 'dp'), may hold values from -0.5 to 0.5
- value_inner: bfloat16 [64, 128, 128], P('tensor', 'dp'), may hold values from -0.5 to 0.5
- value_outer: bfloat16 [64, 128, 128], P('tensor', 'dp'), may hold values from -0.5 to 0.5
- down_inner: bfloat16 [64, 128, 128], P('tensor', 'dp'), may hold values from -0.5 to 0.5
- down_outer: bfloat16 [64, 128, 128], P('tensor', 'dp'), may hold values from -0.5 to 0.5
Outputs:
- mixed: bfloat16 [16384, 8192], P('dp', 'tensor')
- tokens_grad: bfloat16 [16384, 8192], P('dp', 'tensor')
- gate_inner_grad: float32 [64, 128, 128], P('tensor', 'dp')
- gate_outer_grad: float32 [64, 128, 128], P('tensor', 'dp')
- value_inner_grad: float32 [64, 128, 128], P('tensor', 'dp')
- value_outer_grad: float32 [64, 128, 128], P('tensor', 'dp')
- down_inner_grad: float32 [64, 128, 128], P('tensor', 'dp')
- down_outer_grad: float32 [64, 128, 128], P('tensor', 'dp')
All inputs are finite; a program needn't handle non-finite values.
Results may differ from a plain program's by a relative error of at most 0.0072.
Values may be sent and summed in bfloat16 or wider, within the bound.
No kernel may reach another device: no remote copies, remote signals or barrier semaphores. Data moves between devices by JAX's collectives and lax.ppermute only.
A program may use at most 64 MiB of HBM per device.

v0:
```python
import jax
import jax.numpy as jnp
from jax import lax
from jax.sharding import PartitionSpec as P


def blockwise(weights, values):
    return jnp.einsum("tbi,bio->tbo", values, weights, preferred_element_type=jnp.float32)


def blockwise_back(weights, values):
    return jnp.einsum("tbo,bio->tbi", values, weights, preferred_element_type=jnp.float32)


def block_outer(left, right, scale):
    return jnp.einsum("tbi,tbo->bio", left, right, preferred_element_type=jnp.float32) * scale


def spread(values):
    count_tok, count_local, width = values.shape
    total = count_local * lax.axis_size("tensor")
    fold = width // total
    shaped = values.reshape(count_tok, count_local, total, fold)
    return shaped.transpose(0, 2, 1, 3).reshape(count_tok, total, count_local * fold)


def collect(values):
    count_tok, total, piece = values.shape
    count_local = total // lax.axis_size("tensor")
    fold = piece // count_local
    shaped = values.reshape(count_tok, total, count_local, fold)
    return shaped.transpose(0, 2, 1, 3).reshape(count_tok, count_local, total * fold)


def local(
    tokens, cotangent, gate_inner, gate_outer, value_inner, value_outer, down_inner, down_outer
):
    tok_count = tokens.shape[0]
    local_blocks = gate_inner.shape[0]
    width = gate_inner.shape[2]
    scale = float(tok_count * lax.axis_size("dp")) ** (-0.5)
    token_rows = tokens.reshape(tok_count, local_blocks, width)
    cot_rows = cotangent.reshape(tok_count, local_blocks, width)
    w_gate_inner, w_value_inner, w_gate_outer, w_value_outer, w_down_inner, w_down_outer = (
        lax.all_gather(gate_inner, "dp", axis=1, tiled=True),
        lax.all_gather(value_inner, "dp", axis=1, tiled=True),
        lax.all_gather(gate_outer, "dp", axis=1, tiled=True),
        lax.all_gather(value_outer, "dp", axis=1, tiled=True),
        lax.all_gather(down_inner, "dp", axis=1, tiled=True),
        lax.all_gather(down_outer, "dp", axis=1, tiled=True),
    )
    gate_first = blockwise(w_gate_inner, token_rows).astype(jnp.bfloat16)
    value_first = blockwise(w_value_inner, token_rows).astype(jnp.bfloat16)
    gate_mixed = lax.all_to_all(
        spread(gate_first), "tensor", split_axis=1, concat_axis=2, tiled=True
    )
    value_mixed = lax.all_to_all(
        spread(value_first), "tensor", split_axis=1, concat_axis=2, tiled=True
    )
    gate_pre = blockwise(w_gate_outer, gate_mixed)
    value_pre = blockwise(w_value_outer, value_mixed)
    hidden = (jax.nn.silu(gate_pre) * value_pre).astype(jnp.bfloat16)
    gate_mixed, value_mixed, gate_pre, value_pre, hidden = (
        gate_mixed,
        value_mixed,
        gate_pre,
        value_pre,
        hidden,
    )
    down_first = blockwise(w_down_inner, hidden).astype(jnp.bfloat16)
    down_mixed = lax.all_to_all(
        spread(down_first), "tensor", split_axis=1, concat_axis=2, tiled=True
    )
    down_mixed, mixed_rows = (down_mixed, blockwise(w_down_outer, down_mixed).astype(jnp.bfloat16))
    down_send = blockwise_back(w_down_outer, cot_rows).astype(jnp.bfloat16)
    down_back = collect(
        lax.all_to_all(down_send, "tensor", split_axis=2, concat_axis=1, tiled=True)
    )
    down_back, hidden_back = (down_back, blockwise_back(w_down_inner, down_back))
    sigma = jax.nn.sigmoid(gate_pre)
    gate_back = (hidden_back * value_pre * sigma * (1.0 + gate_pre * (1.0 - sigma))).astype(
        jnp.bfloat16
    )
    value_back = (hidden_back * gate_pre * sigma).astype(jnp.bfloat16)
    gate_send = blockwise_back(w_gate_outer, gate_back).astype(jnp.bfloat16)
    value_send = blockwise_back(w_value_outer, value_back).astype(jnp.bfloat16)
    gate_return = collect(
        lax.all_to_all(gate_send, "tensor", split_axis=2, concat_axis=1, tiled=True)
    )
    value_return = collect(
        lax.all_to_all(value_send, "tensor", split_axis=2, concat_axis=1, tiled=True)
    )
    back_rows = (
        blockwise_back(w_gate_inner, gate_return) + blockwise_back(w_value_inner, value_return)
    ).astype(jnp.bfloat16)
    gate_return, value_return, back_rows = (gate_return, value_return, back_rows)
    grads = (
        lax.psum_scatter(
            block_outer(token_rows, gate_return, scale), "dp", scatter_dimension=1, tiled=True
        ),
        lax.psum_scatter(
            block_outer(gate_mixed, gate_back, scale), "dp", scatter_dimension=1, tiled=True
        ),
        lax.psum_scatter(
            block_outer(token_rows, value_return, scale), "dp", scatter_dimension=1, tiled=True
        ),
        lax.psum_scatter(
            block_outer(value_mixed, value_back, scale), "dp", scatter_dimension=1, tiled=True
        ),
        lax.psum_scatter(
            block_outer(hidden, down_back, scale), "dp", scatter_dimension=1, tiled=True
        ),
        lax.psum_scatter(
            block_outer(down_mixed, cot_rows, scale), "dp", scatter_dimension=1, tiled=True
        ),
    )
    (
        grad_gate_inner,
        grad_gate_outer,
        grad_value_inner,
        grad_value_outer,
        grad_down_inner,
        grad_down_outer,
    ) = grads
    return (
        mixed_rows.reshape(tok_count, local_blocks * width),
        back_rows.reshape(tok_count, local_blocks * width),
        grad_gate_inner,
        grad_gate_outer,
        grad_value_inner,
        grad_value_outer,
        grad_down_inner,
        grad_down_outer,
    )


def solution(mesh):
    placed = (
        P("dp", "tensor"),
        P("dp", "tensor"),
        P("tensor", "dp", None),
        P("tensor", "dp", None),
        P("tensor", "dp", None),
        P("tensor", "dp", None),
        P("tensor", "dp", None),
        P("tensor", "dp", None),
    )
    return jax.shard_map(
        local,
        mesh=mesh,
        in_specs=placed,
        out_specs=(
            P("dp", "tensor"),
            P("dp", "tensor"),
            P("tensor", "dp", None),
            P("tensor", "dp", None),
            P("tensor", "dp", None),
            P("tensor", "dp", None),
            P("tensor", "dp", None),
            P("tensor", "dp", None),
        ),
        check_vma=False,
    )
```

profile of v0, /device:TPU:1, one launch (start us, length us, event | category | flops | bytes accessed | tf_op | source)
XLA Modules:
  0.0 1747.9 jit_solution(2581107491195922211)
XLA Ops:
  7.9 71.7 %all_gather.18 = bf16[8,128,128]{2,0,1:T(8,128)(2,1)S(1)} all-gather(bf16[8,2,128]{2,0,1:T(8,128)(2,1)S(1)} %copy.136), channel_id=1, replica_groups=mesh['dp'=64,'tensor'=8] {'dp'}, dimensions={1}, use_global_device_ids=true | all-gather | bytes 266240 | tf_op jit(solution)/shard_map/all_gather | solution.py:45
  81.3 6.5 all-to-all-start
  87.8 60.3 %all_gather.20 = bf16[8,128,128]{2,0,1:T(8,128)(2,1)S(1)} all-gather(bf16[8,2,128]{2,0,1:T(8,128)(2,1)S(1)} %copy.145), channel_id=1, replica_groups=mesh['dp'=64,'tensor'=8] {'dp'}, dimensions={1}, use_global_device_ids=true | all-gather | bytes 266240 | tf_op jit(solution)/shard_map/all_gather | solution.py:46
  149.8 7.0 all-to-all-start.1
  156.9 62.4 %all_gather.23 = bf16[8,128,128]{2,0,1:T(8,128)(2,1)S(1)} all-gather(bf16[8,2,128]{2,0,1:T(8,128)(2,1)S(1)} %copy.159), channel_id=1, replica_groups=mesh['dp'=64,'tensor'=8] {'dp'}, dimensions={1}, use_global_device_ids=true | all-gather | bytes 266240 | tf_op jit(solution)/shard_map/all_gather | solution.py:50
  221.5 6.9 all-to-all-start.3
  229.8 65.4 %all_gather.22 = bf16[8,128,128]{2,0,1:T(8,128)(2,1)} all-gather(bf16[8,2,128]{2,0,1:T(8,128)(2,1)S(1)} %copy.154), channel_id=1, replica_groups=mesh['dp'=64,'tensor'=8] {'dp'}, dimensions={1}, use_global_device_ids=true | all-gather | bytes 266240 | tf_op jit(solution)/shard_map/all_gather | solution.py:49
  295.2 61.9 %all_gather.21 = bf16[8,128,128]{2,0,1:T(8,128)(2,1)S(1)} all-gather(bf16[8,2,128]{2,0,1:T(8,128)(2,1)S(1)} %copy.151), channel_id=1, replica_groups=mesh['dp'=64,'tensor'=8] {'dp'}, dimensions={1}, use_global_device_ids=true | all-gather | bytes 266240 | tf_op jit(solution)/shard_map/all_gather | solution.py:48
  357.1 60.2 %all_gather.19 = bf16[8,128,128]{2,0,1:T(8,128)(2,1)S(1)} all-gather(bf16[8,2,128]{2,0,1:T(8,128)(2,1)S(1)} %copy.142), channel_id=1, replica_groups=mesh['dp'=64,'tensor'=8] {'dp'}, dimensions={1}, use_global_device_ids=true | all-gather | bytes 266240 | tf_op jit(solution)/shard_map/all_gather | solution.py:47
  420.6 2.2 copy.168
  424.3 1.8 multiply_convert_fusion
  428.0 1.3 convolution_multiply_fusion.4
  429.4 1.1 copy.187
  431.8 1.1 copy.191
  434.0 2.1 fusion.3
  436.1 1.2 reshape.72
  437.7 17.1 all_to_all.99
  455.1 1.1 copy.196
  457.0 13.9 all_to_all.100
  475.1 12.1 all_to_all.101
  492.6 150.2 %reduce-scatter.15.cloned.1.call-done = f32[8,2,128]{2,0,1:T(8,128)} async-done(((f32[8,128,128]{2,0,1:T(8,128)}), f32[8,2,128]{2,0,1:T(8,128)}) %reduce-scatter.15.cloned.1.call-update) | async-done | bytes 8208 | tf_op jit(solution)/shard_map/reduce_scatter | solution.py:110
  642.9 1.3 copy.203
  644.2 217.9 %reduce-scatter.9.cloned.1.call-done = f32[8,2,128]{2,0,1:T(8,128)} async-done(((f32[8,128,128]{2,0,1:T(8,128)}), f32[8,2,128]{2,0,1:T(8,128)}) %reduce-scatter.9.cloned.1.call-update) | async-done | bytes 8208 | tf_op jit(solution)/shard_map/reduce_scatter | solution.py:101
  862.0 1.3 copy.200
  863.3 218.1 %reduce-scatter.13.cloned.1.call-done = f32[8,2,128]{2,0,1:T(8,128)} async-done(((f32[8,128,128]{2,0,1:T(8,128)}), f32[8,2,128]{2,0,1:T(8,128)}) %reduce-scatter.13.cloned.1.call-update) | async-done | bytes 8208 | tf_op jit(solution)/shard_map/reduce_scatter | solution.py:107
  1081.5 1.3 copy.202
  1082.8 218.2 %reduce-scatter.17.cloned.1.call-done = f32[8,2,128]{2,0,1:T(8,128)} async-done(((f32[8,128,128]{2,0,1:T(8,128)}), f32[8,2,128]{2,0,1:T(8,128)}) %reduce-scatter.17.cloned.1.call-update) | async-done | bytes 8208 | tf_op jit(solution)/shard_map/reduce_scatter | solution.py:113
  1301.0 1.3 copy.204
  1302.3 218.0 %reduce-scatter.11.cloned.1.call-done = f32[8,2,128]{2,0,1:T(8,128)} async-done(((f32[8,128,128]{2,0,1:T(8,128)}), f32[8,2,128]{2,0,1:T(8,128)}) %reduce-scatter.11.cloned.1.call-update) | async-done | bytes 8208 | tf_op jit(solution)/shard_map/reduce_scatter | solution.py:104
  1520.3 1.3 copy.201
  1521.6 218.2 %reduce-scatter.7.cloned.1.call-done = f32[8,2,128]{2,0,1:T(8,128)} async-done(((f32[8,128,128]{2,0,1:T(8,128)}), f32[8,2,128]{2,0,1:T(8,128)}) %reduce-scatter.7.cloned.1.call-update) | async-done | bytes 8208 | tf_op jit(solution)/shard_map/reduce_scatter | solution.py:98
  1739.8 1.3 copy.199
  (95 shorter events, 27.7 us)
Async XLA Ops:
  7.2 72.4 %copy-start = (bf16[256,1024]{1,0:T(8,128)(2,1)S(1)}, bf16[256,1024]{1,0:T(8,128)(2,1)}, u32[]{:S(2)}) copy-start(bf16[256,1024]{1,0:T(8,128)(2,1)} %param.8) | copy-start | bytes 1572868
  81.3 6.5 copy-start.12
  81.3 68.5 %all-to-all-start = ((bf16[256,64,16]{0,2,1:T(8,128)(2,1)}), bf16[256,64,16]{0,2,1:T(8,128)(2,1)S(1)}, u32[]{:S(2)}, u32[]{:S(2)}) async-start(bf16[256,64,16]{0,2,1:T(8,128)(2,1)} %copy.140), calls=%async_computation | async-start | bytes 1048576 | tf_op jit(solution)/shard_map/all_to_all | solution.py:54
  149.8 7.0 copy-start.13
  149.8 69.5 %copy-start.1 = (bf16[256,1024]{1,0:T(8,128)(2,1)S(1)}, bf16[256,1024]{1,0:T(8,128)(2,1)}, u32[]{:S(2)}) copy-start(bf16[256,1024]{1,0:T(8,128)(2,1)} %param.9) | copy-start | bytes 1572868
  149.8 70.9 %all-to-all-start.1 = ((bf16[256,64,16]{0,2,1:T(8,128)(2,1)}), bf16[256,64,16]{0,2,1:T(8,128)(2,1)S(1)}, u32[]{:S(2)}, u32[]{:S(2)}) async-start(bf16[256,64,16]{0,2,1:T(8,128)(2,1)} %copy.149), calls=%async_computation.1 | async-start | bytes 1048576 | tf_op jit(solution)/shard_map/all_to_all | solution.py:57
  220.7 7.8 copy-start.14
  220.7 0.8 copy-start.7
  221.5 196.9 %all-to-all-start.3 = ((bf16[256,8,128]{0,1,2:T(8,128)(2,1)}), bf16[256,8,128]{0,1,2:T(8,128)(2,1)}, u32[]{:S(2)}, u32[]{:S(2)}) async-start(bf16[256,8,128]{0,1,2:T(8,128)(2,1)} %copy.164), calls=%async_computation.3 | async-start | bytes 1048576 | tf_op jit(solution)/shard_map/all_to_all | solution.py:77
  228.4 0.7 copy-start.15
  228.4 414.4 %reduce-scatter.15.cloned.1.call-start = ((), (), s32[]{:S(2)}) async-start(), calls=%async_computation.16 | async-start | bytes 532480 | tf_op jit(solution)/shard_map/reduce_scatter | solution.py:110
  229.1 0.7 copy-start.16
  417.3 1.0 copy-start.8
  423.2 1.0 copy-start.6
  423.2 1.1 copy-start.11
  426.1 0.8 copy-start.4
  428.0 434.0 %reduce-scatter.9.cloned.1.call-start = ((), (), s32[]{:S(2)}) async-start(), calls=%async_computation.13 | async-start | bytes 532480 | tf_op jit(solution)/shard_map/reduce_scatter | solution.py:101
  430.5 1.0 copy-start.3
  430.5 650.9 %reduce-scatter.13.cloned.1.call-start = ((), (), s32[]{:S(2)}) async-start(), calls=%async_computation.15 | async-start | bytes 532480 | tf_op jit(solution)/shard_map/reduce_scatter | solution.py:107
  432.9 1.0 copy-start.5
  433.0 868.0 %reduce-scatter.17.cloned.1.call-start = ((), (), s32[]{:S(2)}) async-start(), calls=%async_computation.17 | async-start | bytes 532480 | tf_op jit(solution)/shard_map/reduce_scatter | solution.py:113
  456.2 1064.0 %reduce-scatter.11.cloned.1.call-start = ((), (), s32[]{:S(2)}) async-start(), calls=%async_computation.14 | async-start | bytes 532480 | tf_op jit(solution)/shard_map/reduce_scatter | solution.py:104
  471.3 0.8 copy-start.9
  473.4 1.0 copy-start.2
  473.4 1266.4 %reduce-scatter.7.cloned.1.call-start = ((), (), s32[]{:S(2)}) async-start(), calls=%async_computation.12 | async-start | bytes 532480 | tf_op jit(solution)/shard_map/reduce_scatter | solution.py:98
  490.3 1.0 copy-start.10
Sparse Core Ops, SparseCore 0:
  428.1 214.7 reduce-scatter.14
  645.9 216.1 reduce-scatter.8
  864.8 216.6 reduce-scatter.12
  1084.3 216.6 reduce-scatter.16
  1303.6 216.6 reduce-scatter.10
  1523.1 216.6 reduce-scatter.6
where the time goes:
time: 1750 us
  waiting for transfers between devices  1240 us (71%)
  blocking collectives  425 us (24%)
  local copies, waits for them, and re-layouts  37 us (2%)
  starting transfers between devices  20.9 us (1%)
    reduce_scatter x1, waiting for transfers between devices, local(): lax.psum_scatter(block_outer(down_mixed, cot_rows, scale), 'dp', scatter_...  218 us
    reduce_scatter x1, waiting for transfers between devices, local(): lax.psum_scatter(block_outer(token_rows, gate_return, scale), 'dp', scatt...  218 us
    reduce_scatter x1, waiting for transfers between devices, local(): lax.psum_scatter(block_outer(value_mixed, value_back, scale), 'dp', scatt...  218 us
    reduce_scatter x1, waiting for transfers between devices, local(): lax.psum_scatter(block_outer(token_rows, value_return, scale), 'dp', scat...  218 us
    reduce_scatter x1, waiting for transfers between devices, local(): lax.psum_scatter(block_outer(gate_mixed, gate_back, scale), 'dp', scatter...  218 us
    reduce_scatter x1, waiting for transfers between devices, local(): lax.psum_scatter(block_outer(hidden, down_back, scale), 'dp', scatter_dim...  150 us
    all_gather x1, blocking collectives, local(): lax.all_gather(gate_inner, 'dp', axis=1, tiled=True)  71.7 us
    all_gather x1, blocking collectives, local(): lax.all_gather(down_inner, 'dp', axis=1, tiled=True)  65.4 us
  transfers between devices with their start and end apart: 9, of which 6 were waited for; matrix products, arithmetic and copies ran while one was open for 2% of the time, Pallas kernels for 0%

commit v1 on v0

v1 whole, which is shorter than its diff:
```python
import functools

import jax
import jax.numpy as jnp
from jax import lax
from jax.experimental import pallas as pl
from jax.experimental.pallas import tpu as pltpu
from jax.sharding import Mesh, PartitionSpec as P

BF = jnp.bfloat16
F32 = jnp.float32
AXES = ("xlo", "z", "core", "xhi", "y")
QUAD = ("xlo", "core")
PLANE = ("xhi", "y", "xlo", "core")
DP = ("xlo", "z", "core")
WIDTH = 128
PAIR = 256
TOK = 256
SLAB = 1024


def dot(left, right, left_dim, right_dim):
    return lax.dot_general(
        left, right, (((left_dim,), (right_dim,)), ((), ())), preferred_element_type=F32
    )


def one_hot(shape, test):
    rows = lax.broadcasted_iota(jnp.int32, shape, 0)
    cols = lax.broadcasted_iota(jnp.int32, shape, 1)
    return jnp.where(test(rows, cols), 1.0, 0.0).astype(BF)


def pairs_from_natural():
    return one_hot(
        (PAIR, PAIR),
        lambda r, c: c == ((r >> 1) & 1) * WIDTH + (r >> 2) * 2 + (r & 1),
    )


def natural_from_pairs():
    return one_hot(
        (PAIR, PAIR),
        lambda r, c: r == ((c >> 1) & 1) * WIDTH + (c >> 2) * 2 + (c & 1),
    )


def quads_from_natural():
    return one_hot(
        (PAIR, PAIR),
        lambda r, c: c == ((r >> 2) & 1) * WIDTH + (r >> 3) * 4 + (r & 3),
    )


def gathered_to_pairs(count_z):
    def test(r, c):
        inner = r & 7
        zed = (r >> 3) & (count_z - 1)
        xlo = (r >> 3) // count_z
        return c == (zed * 2 + xlo) * 8 + inner

    return one_hot((PAIR, PAIR), test)


def expand(factor):
    rows = lax.broadcasted_iota(jnp.int32, factor.shape, 0)
    first = ((rows >> 1) & 1) == 0
    zero = jnp.zeros_like(factor)
    return jnp.concatenate(
        [jnp.where(first, factor, zero), jnp.where(first, zero, factor)], axis=1
    )


def own_block(full):
    rows = lax.broadcasted_iota(jnp.int32, (PAIR, WIDTH), 0)
    return jnp.where(((rows >> 1) & 1) == 0, full[:, :WIDTH], full[:, WIDTH:])


def factor_of(rows, index):
    return expand(rows[:, index * WIDTH : (index + 1) * WIDTH])


def split_kernel(tok_ref, cot_ref, out_ref):
    for part in range(4):
        cols = slice(part * PAIR, (part + 1) * PAIR)
        out_ref[2 * part * TOK : (2 * part + 1) * TOK, :] = tok_ref[:, cols]
        out_ref[(2 * part + 1) * TOK : (2 * part + 2) * TOK, :] = cot_ref[:, cols]


def first_kernel(count_z, weights_ref, rows_ref, send_ref, weights_out_ref):
    weights = dot(gathered_to_pairs(count_z), weights_ref[...], 1, 0).astype(BF)
    weights_out_ref[...] = weights
    nat = natural_from_pairs()
    quads = quads_from_natural()
    gate = dot(quads, dot(nat, factor_of(weights, 0), 1, 0).astype(BF), 1, 1).astype(BF)
    value = dot(quads, dot(nat, factor_of(weights, 2), 1, 0).astype(BF), 1, 1).astype(BF)
    down = factor_of(weights, 5)
    for part in range(4):
        tok = rows_ref[2 * part * TOK : (2 * part + 1) * TOK, :]
        cot = rows_ref[(2 * part + 1) * TOK : (2 * part + 2) * TOK, :]
        at = part * TOK
        send_ref[:, at : at + TOK] = dot(gate, tok, 1, 1).astype(BF)
        send_ref[:, SLAB + at : SLAB + at + TOK] = dot(value, tok, 1, 1).astype(BF)
        send_ref[:, 2 * SLAB + at : 2 * SLAB + at + TOK] = dot(down, cot, 1, 1).astype(BF)


def middle_kernel(weights_ref, recv_ref, send_ref, grad_ref, hid_ref, gate_ref, value_ref):
    pairs = pairs_from_natural()
    quads = quads_from_natural()
    weights = weights_ref[...]
    gate_w = factor_of(weights, 1)
    value_w = factor_of(weights, 3)
    down_w = factor_of(weights, 4)
    gate_fwd = dot(pairs, gate_w, 1, 1).astype(BF)
    value_fwd = dot(pairs, value_w, 1, 1).astype(BF)
    gate_bwd = dot(gate_w, pairs, 1, 1).astype(BF)
    value_bwd = dot(value_w, pairs, 1, 1).astype(BF)
    down_fwd = dot(quads, down_w, 1, 1).astype(BF)
    down_bwd = dot(down_w, quads, 1, 1).astype(BF)
    for part in range(4):
        at = part * TOK
        cols = slice(at, at + TOK)
        gate_pre = dot(gate_fwd, recv_ref[:, cols], 1, 0)
        value_pre = dot(value_fwd, recv_ref[:, SLAB + at : SLAB + at + TOK], 1, 0)
        sigma = jax.nn.sigmoid(gate_pre)
        hidden = (gate_pre * sigma * value_pre).astype(BF)
        hid_ref[:, cols] = hidden
        send_ref[:, cols] = dot(down_fwd, hidden, 1, 0).astype(BF)
        back = dot(down_bwd, recv_ref[:, 2 * SLAB + at : 2 * SLAB + at + TOK], 1, 0)
        gate_back = (back * value_pre * sigma * (1.0 + gate_pre * (1.0 - sigma))).astype(BF)
        value_back = (back * gate_pre * sigma).astype(BF)
        gate_ref[:, cols] = gate_back
        value_ref[:, cols] = value_back
        send_ref[:, SLAB + at : SLAB + at + TOK] = dot(gate_bwd, gate_back, 1, 0).astype(BF)
        send_ref[:, 2 * SLAB + at : 2 * SLAB + at + TOK] = dot(
            value_bwd, value_back, 1, 0
        ).astype(BF)
    gate_grad = dot(recv_ref[:, :SLAB], gate_ref[...], 1, 1).astype(BF)
    value_grad = dot(recv_ref[:, SLAB : 2 * SLAB], value_ref[...], 1, 1).astype(BF)
    down_grad = dot(hid_ref[...], recv_ref[:, 2 * SLAB :], 1, 1).astype(BF)
    grad_ref[:, :WIDTH] = own_block(dot(gate_grad, pairs, 1, 0)).astype(BF)
    grad_ref[:, WIDTH : 2 * WIDTH] = own_block(dot(value_grad, pairs, 1, 0)).astype(BF)
    grad_ref[:, 2 * WIDTH :] = own_block(dot(down_grad, quads, 1, 0)).astype(BF)


def last_kernel(
    weights_ref, rows_ref, recv_ref, outer_ref, out_ref, grad_ref, left_ref, cot_ref
):
    pairs = pairs_from_natural()
    nat = natural_from_pairs()
    quads = quads_from_natural()
    weights = weights_ref[...]
    down = factor_of(weights, 5)
    gate = dot(nat, dot(factor_of(weights, 0), quads, 1, 1).astype(BF), 1, 0).astype(BF)
    value = dot(nat, dot(factor_of(weights, 2), quads, 1, 1).astype(BF), 1, 0).astype(BF)
    for part in range(4):
        at = part * TOK
        tok = rows_ref[2 * part * TOK : (2 * part + 1) * TOK, :]
        cot_ref[at : at + TOK, :] = rows_ref[(2 * part + 1) * TOK : (2 * part + 2) * TOK, :]
        left_ref[:, at : at + TOK] = dot(pairs, tok, 1, 1).astype(BF)
        mixed = dot(recv_ref[:, at : at + TOK], down, 0, 0)
        out_ref[2 * part * TOK : (2 * part + 1) * TOK, :] = mixed.astype(BF)
        back = dot(gate, recv_ref[:, SLAB + at : SLAB + at + TOK], 1, 0) + dot(
            value, recv_ref[:, 2 * SLAB + at : 2 * SLAB + at + TOK], 1, 0
        )
        out_ref[(2 * part + 1) * TOK : (2 * part + 2) * TOK, :] = back.T.astype(BF)
    gate_grad = dot(left_ref[...], recv_ref[:, SLAB : 2 * SLAB], 1, 1).astype(BF)
    value_grad = dot(left_ref[...], recv_ref[:, 2 * SLAB :], 1, 1).astype(BF)
    down_grad = dot(recv_ref[:, :SLAB], cot_ref[...], 1, 0)
    inner = jnp.concatenate(
        [
            own_block(dot(gate_grad, quads, 1, 0)).astype(BF),
            own_block(dot(value_grad, quads, 1, 0)).astype(BF),
            own_block(down_grad).astype(BF),
        ],
        axis=1,
    )
    for half in range(2):
        take = lambda group: one_hot(
            (PAIR, PAIR),
            lambda r, c: (((r >> 2) & 1) == group)
            & (c == half * WIDTH + (r >> 3) * 4 + (r & 3)),
        )
        grad_ref[half * PAIR : (half + 1) * PAIR, :] = (
            dot(take(0), outer_ref[...], 1, 0) + dot(take(1), inner, 1, 0)
        ).astype(BF)


def end_kernel(count_z, scale, rows_ref, grads_ref, mixed_ref, back_ref, *grad_refs):
    def test(r, c):
        inner = c & 3
        group = (c >> 2) & 1
        core = (c >> 3) & 1
        xlo = (c >> 4) // count_z
        return r == group * 16 + xlo * 8 + core * 4 + inner

    total = dot(one_hot((32, 2 * PAIR), test), grads_ref[...], 1, 0) * scale
    for group in range(2):
        for third in range(3):
            for block in range(8):
                row = group * 16 + block * 2
                grad_refs[group * 3 + third][block] = total[
                    row : row + 2, third * WIDTH : (third + 1) * WIDTH
                ]
    for part in range(4):
        cols = slice(part * PAIR, (part + 1) * PAIR)
        mixed_ref[:, cols] = rows_ref[2 * part * TOK : (2 * part + 1) * TOK, :]
        back_ref[:, cols] = rows_ref[(2 * part + 1) * TOK : (2 * part + 2) * TOK, :]


def call(kernel, name, outs, scratch=()):
    return pl.pallas_call(
        kernel,
        out_shape=outs,
        scratch_shapes=list(scratch),
        compiler_params=pltpu.CompilerParams(vmem_limit_bytes=40 * 1024 * 1024),
        name=name,
    )


def shape(dims, kind=BF):
    return jax.ShapeDtypeStruct(dims, kind)


def local(
    tokens, cotangent, gate_inner, gate_outer, value_inner, value_outer, down_inner, down_outer
):
    count_z = lax.axis_size("z")
    scale = float(tokens.shape[0] * lax.axis_size(DP)) ** (-0.5)
    quad = lax.axis_index(QUAD)

    mine = jnp.concatenate(
        [gate_inner, gate_outer, value_inner, value_outer, down_inner, down_outer], axis=0
    )
    near = lax.all_gather(mine, QUAD, axis=0, tiled=True).reshape(4, 6, 8, 2, WIDTH)
    near = lax.dynamic_slice_in_dim(near, quad * 2, 2, 2)
    near = near.transpose(0, 2, 3, 1, 4).reshape(16, 6 * WIDTH)

    rows = call(split_kernel, "split", shape((8 * TOK, PAIR)))(tokens, cotangent)
    rows = lax.all_to_all(rows, QUAD, split_axis=0, concat_axis=0, tiled=True)
    gathered = lax.all_gather(near, "z", axis=0, tiled=True)

    send, weights = call(
        functools.partial(first_kernel, count_z),
        "first",
        (shape((PAIR, 3 * SLAB)), shape((PAIR, 6 * WIDTH))),
    )(gathered, rows)
    recv = lax.all_to_all(send, PLANE, split_axis=0, concat_axis=0, tiled=True)
    send, outer_grads = call(
        middle_kernel,
        "middle",
        (shape((PAIR, 3 * SLAB)), shape((PAIR, 3 * WIDTH))),
        [pltpu.VMEM((PAIR, SLAB), BF)] * 3,
    )(weights, recv)
    recv = lax.all_to_all(send, PLANE, split_axis=0, concat_axis=0, tiled=True)
    out_rows, grads = call(
        last_kernel,
        "last",
        (shape((8 * TOK, PAIR)), shape((2 * PAIR, 3 * WIDTH))),
        [pltpu.VMEM((PAIR, SLAB), BF), pltpu.VMEM((SLAB, PAIR), BF)],
    )(weights, rows, recv, outer_grads)
    out_rows = lax.all_to_all(out_rows, QUAD, split_axis=0, concat_axis=0, tiled=True)
    grads = lax.all_to_all(grads, DP, split_axis=0, concat_axis=0, tiled=True)
    mixed, back, g_gate_o, g_value_o, g_down_i, g_gate_i, g_value_i, g_down_o = call(
        functools.partial(end_kernel, count_z, scale),
        "end",
        (shape((TOK, 4 * PAIR)),) * 2 + (shape((8, 2, WIDTH), F32),) * 6,
    )(out_rows, grads)
    return mixed, back, g_gate_i, g_gate_o, g_value_i, g_value_o, g_down_i, g_down_o


def solution(mesh):
    fine = Mesh(mesh.devices.reshape(2, 16, 2, 2, 4), AXES)
    rows = P(DP, ("xhi", "y"))
    factor = P(("xhi", "y"), DP, None)
    return jax.shard_map(
        local,
        mesh=fine,
        in_specs=(rows,) * 2 + (factor,) * 6,
        out_specs=(rows,) * 2 + (factor,) * 6,
        check_vma=False,
    )
```

time: 1750 us -> 178 us (0.10)
  waiting for transfers between devices: 1240 us -> 0.01 us
  blocking collectives: 425 us -> 156 us
  local copies, waits for them, and re-layouts: 37 us -> 2.21 us
    reduce_scatter x6 -> x0, waiting for transfers between devices: 1240 us -> none  [the longest x1 218 us: local(): lax.psum_scatter(block_outer(down_mixed, cot_rows, scale), 'dp', scatter_...]
    all_gather x6 -> x2, blocking collectives: 382 us -> 40.9 us  [the longest x1 25.4 us: local(): gathered = lax.all_gather(near, 'z', axis=0, tiled=True)]
    all_to_all x3 -> x4, blocking collectives: 43.1 us -> 115 us  [the longest x2 63.1 us: local(): recv = lax.all_to_all(send, PLANE, split_axis=0, concat_axis=0, tiled=True)]
  transfers between devices with their start and end apart: 9 -> 1, of which waited for: 6 -> 0; matrix products, arithmetic and copies ran while one was open for 2% -> 0% of each run, Pallas kernels for 0% -> 0%
where the time goes in v1:
time: 178 us
  blocking collectives  156 us (88%)
  starting transfers between devices  10.5 us (6%)
  Pallas kernels  8.04 us (5%)
  local copies, waits for them, and re-layouts  2.21 us (1%)
    all_to_all x2, blocking collectives, local(): recv = lax.all_to_all(send, PLANE, split_axis=0, concat_axis=0, tiled=True)  63.1 us
    all_to_all x1, blocking collectives, local(): grads = lax.all_to_all(grads, DP, split_axis=0, concat_axis=0, tiled=True)  35.6 us
    all_gather x1, blocking collectives, local(): gathered = lax.all_gather(near, 'z', axis=0, tiled=True)  25.4 us
    all_to_all x1, blocking collectives, local(): lax.all_to_all(out_rows, QUAD, split_axis=0, concat_axis=0, tiled=True)  16.5 us
    all_gather x1, blocking collectives, local(): lax.all_gather(mine, QUAD, axis=0, tiled=True).reshape(4, 6, 8, 2, WIDTH)  15.5 us
    all_to_all x1, starting transfers between devices, local(): rows = lax.all_to_all(rows, QUAD, split_axis=0, concat_axis=0, tiled=True)  10.5 us
  transfers between devices with their start and end apart: 1, of which 0 were waited for; matrix products, arithmetic and copies ran while one was open for 0% of the time, Pallas kernels for 0%

profile of v1, /device:TPU:1, one launch (start us, length us, event | category | flops | bytes accessed | tf_op | source)
XLA Modules:
  0.0 177.6 jit_solution(8524765056693489699)
XLA Ops:
  0.6 0.0 copy-start
  0.6 1.0 copy-done
  1.7 0.0 copy-start.1
  1.7 1.0 copy-done.1
  2.7 1.0 split.1
  3.8 0.0 copy-start.2
  3.8 0.0 copy-start.3
  3.8 0.0 copy-start.4
  3.8 0.0 copy-start.5
  3.8 0.0 copy-start.6
  3.8 0.0 copy-start.7
  3.8 10.5 %all-to-all-start = ((bf16[4,512,256]{2,1,0:T(8,128)(2,1)}), bf16[4,512,256]{2,1,0:T(8,128)(2,1)S(1)}, u32[]{:S(2)}, u32[]{:S(2)}) async-start(bf16[4,512,256]{2,1,0:T(8,128)(2,1)} %bitcast.2), calls=%async_computation | async-start | bytes 2097152 | tf_op jit(solution)/shard_map/all_to_all | solution.py:240
  14.3 0.0 copy-done.2
  14.3 0.0 copy-done.3
  14.3 0.0 copy-done.4
  14.4 0.0 copy-done.5
  14.4 0.0 copy-done.6
  14.4 0.0 copy-done.7
  14.4 15.5 %all_gather.6 = bf16[192,2,128]{2,1,0:T(2,128)(2,1)S(1)} all-gather(bf16[48,2,128]{2,1,0:T(2,128)(2,1)S(1)} %constant_dynamic-update-slice_fusion), channel_id=1, replica_groups=mesh['xlo'=2,'z'=16,'core'=2,'xhi'=2,'y'=4] {'xlo','core'}, dimensions={0}, use_global_device_ids=true | all-gather | bytes 122880 | tf_op jit(solution)/shard_map/all_gather | solution.py:235
  30.0 25.4 %all_gather.7.weights_ref = bf16[256,768]{1,0:T(8,128)(2,1)S(1)} all-gather(bf16[16,768]{1,0:T(8,128)(2,1)S(1)} %bitcast.29), channel_id=1, replica_groups=mesh['xlo'=2,'z'=16,'core'=2,'xhi'=2,'y'=4] {'z'}, dimensions={0}, use_global_device_ids=true | all-gather | bytes 417792 | tf_op jit(solution)/shard_map/all_gather | solution.py:241
  55.4 0.0 all-to-all-done
  55.4 1.2 first.1
  56.5 36.5 %all_to_all.55 = bf16[32,8,3072]{2,1,0:T(8,128)(2,1)S(1)} all-to-all(bf16[32,8,3072]{2,1,0:T(8,128)(2,1)S(1)} %bitcast.22), channel_id=1, replica_groups=mesh['xlo'=2,'z'=16,'core'=2,'xhi'=2,'y'=4] {'xhi','y','xlo','core'}, dimensions={0} | all-to-all | bytes 3145728 | tf_op jit(solution)/shard_map/all_to_all | solution.py:248
  93.1 2.6 %middle.1 = (bf16[256,3072]{1,0:T(8,128)(2,1)S(1)}, bf16[256,384]{1,0:T(8,128)(2,1)S(1)}) custom-call(bf16[256,768]{1,0:T(8,128)(2,1)S(1)} %get-tuple-element.22.weights_ref, bf16[256,3072]{1,0:T(8,128)(2,1)S(1)} %bitcast.20), custom_call_target="tpu_custom_call" | custom-call | tf_op jit(solution)/shard_map/middle/pallas_call | solution.py:249
  95.7 26.6 %all_to_all.56 = bf16[32,8,3072]{2,1,0:T(8,128)(2,1)S(1)} all-to-all(bf16[32,8,3072]{2,1,0:T(8,128)(2,1)S(1)} %bitcast.23), channel_id=1, replica_groups=mesh['xlo'=2,'z'=16,'core'=2,'xhi'=2,'y'=4] {'xhi','y','xlo','core'}, dimensions={0} | all-to-all | bytes 3145728 | tf_op jit(solution)/shard_map/all_to_all | solution.py:255
  122.3 2.1 %last.1 = (bf16[2048,256]{1,0:T(8,128)(2,1)S(1)}, bf16[512,384]{1,0:T(8,128)(2,1)S(1)}) custom-call(bf16[256,768]{1,0:T(8,128)(2,1)S(1)} %get-tuple-element.22.weights_ref, bf16[2048,256]{1,0:T(8,128)(2,1)S(1)} %bitcast.18, bf16[256,3072]{1,0:T(8,128)(2,1)S(1)} %bitcast.19, bf16[256,384]{1,0:T(8,128)(2,1)S(1)} %get-tuple-element.25.outer_ref), custom_call_target="tpu_custom_call" | custom-call | tf_op jit(solution)/shard_map/last/pallas_call | solution.py:256
  124.4 16.5 %all_to_all.57 = bf16[4,512,256]{2,1,0:T(8,128)(2,1)S(1)} all-to-all(bf16[4,512,256]{2,1,0:T(8,128)(2,1)S(1)} %bitcast.25), channel_id=1, replica_groups=mesh['xlo'=2,'z'=16,'core'=2,'xhi'=2,'y'=4] {'xlo','core'}, dimensions={0} | all-to-all | bytes 2097152 | tf_op jit(solution)/shard_map/all_to_all | solution.py:262
  140.9 35.6 %all_to_all.58 = bf16[64,8,384]{2,1,0:T(8,128)(2,1)S(1)} all-to-all(bf16[64,8,384]{2,1,0:T(8,128)(2,1)S(1)} %bitcast.26), channel_id=1, replica_groups=mesh['xlo'=2,'z'=16,'core'=2,'xhi'=2,'y'=4] {'xlo','z','core'}, dimensions={0} | all-to-all | bytes 786432 | tf_op jit(solution)/shard_map/all_to_all | solution.py:263
  176.6 1.1 end.1
  (9 shorter events, 0.1 us)
Async XLA Ops:
  0.6 1.0 copy-start
  1.7 1.0 copy-start.1
  3.8 10.5 %copy-start.2 = (bf16[8,2,128]{2,1,0:T(2,128)(2,1)S(1)}, bf16[8,2,128]{2,1,0:T(2,128)(2,1)}, u32[]{:S(2)}) copy-start(bf16[8,2,128]{2,1,0:T(2,128)(2,1)} %param.10) | copy-start | bytes 12292
  3.8 10.6 %copy-start.3 = (bf16[8,2,128]{2,1,0:T(2,128)(2,1)S(1)}, bf16[8,2,128]{2,1,0:T(2,128)(2,1)}, u32[]{:S(2)}) copy-start(bf16[8,2,128]{2,1,0:T(2,128)(2,1)} %param.11) | copy-start | bytes 12292
  3.8 10.6 %copy-start.4 = (bf16[8,2,128]{2,1,0:T(2,128)(2,1)S(1)}, bf16[8,2,128]{2,1,0:T(2,128)(2,1)}, u32[]{:S(2)}) copy-start(bf16[8,2,128]{2,1,0:T(2,128)(2,1)} %param.12) | copy-start | bytes 12292
  3.8 10.6 %copy-start.5 = (bf16[8,2,128]{2,1,0:T(2,128)(2,1)S(1)}, bf16[8,2,128]{2,1,0:T(2,128)(2,1)}, u32[]{:S(2)}) copy-start(bf16[8,2,128]{2,1,0:T(2,128)(2,1)} %param.13) | copy-start | bytes 12292
  3.8 10.6 %copy-start.6 = (bf16[8,2,128]{2,1,0:T(2,128)(2,1)S(1)}, bf16[8,2,128]{2,1,0:T(2,128)(2,1)}, u32[]{:S(2)}) copy-start(bf16[8,2,128]{2,1,0:T(2,128)(2,1)} %param.14) | copy-start | bytes 12292
  3.8 10.6 %copy-start.7 = (bf16[8,2,128]{2,1,0:T(2,128)(2,1)S(1)}, bf16[8,2,128]{2,1,0:T(2,128)(2,1)}, u32[]{:S(2)}) copy-start(bf16[8,2,128]{2,1,0:T(2,128)(2,1)} %param.15) | copy-start | bytes 12292
  3.8 51.6 %all-to-all-start = ((bf16[4,512,256]{2,1,0:T(8,128)(2,1)}), bf16[4,512,256]{2,1,0:T(8,128)(2,1)S(1)}, u32[]{:S(2)}, u32[]{:S(2)}) async-start(bf16[4,512,256]{2,1,0:T(8,128)(2,1)} %bitcast.2), calls=%async_computation | async-start | bytes 2097152 | tf_op jit(solution)/shard_map/all_to_all | solution.py:240

commit v2 on v1

--- a/solution.py
+++ b/solution.py
@@ -80,11 +80,15 @@
     return expand(rows[:, index * WIDTH : (index + 1) * WIDTH])
 
 
-def split_kernel(tok_ref, cot_ref, out_ref):
+def pack_kernel(*refs):
+    sources, (rows_ref, stack_ref) = refs[:8], refs[8:]
+    for at, ref in enumerate(sources[2:]):
+        stack_ref[at * 8 : (at + 1) * 8] = ref[...]
     for part in range(4):
         cols = slice(part * PAIR, (part + 1) * PAIR)
-        out_ref[2 * part * TOK : (2 * part + 1) * TOK, :] = tok_ref[:, cols]
-        out_ref[(2 * part + 1) * TOK : (2 * part + 2) * TOK, :] = cot_ref[:, cols]
+        for which in range(2):
+            at = (2 * part + which) * TOK
+            rows_ref[at : at + TOK, :] = sources[which][:, cols]
 
 
 def first_kernel(count_z, weights_ref, rows_ref, send_ref, weights_out_ref):
@@ -143,27 +147,22 @@
     grad_ref[:, 2 * WIDTH :] = own_block(dot(down_grad, quads, 1, 0)).astype(BF)
 
 
-def last_kernel(
-    weights_ref, rows_ref, recv_ref, outer_ref, out_ref, grad_ref, left_ref, cot_ref
-):
+def owner_rows(half, group):
+    return one_hot(
+        (PAIR, PAIR),
+        lambda r, c: (((r >> 2) & 1) == group)
+        & (c == half * WIDTH + (r >> 3) * 4 + (r & 3)),
+    )
+
+
+def inner_kernel(rows_ref, recv_ref, outer_ref, grad_ref, left_ref, cot_ref):
+    quads = quads_from_natural()
     pairs = pairs_from_natural()
-    nat = natural_from_pairs()
-    quads = quads_from_natural()
-    weights = weights_ref[...]
-    down = factor_of(weights, 5)
-    gate = dot(nat, dot(factor_of(weights, 0), quads, 1, 1).astype(BF), 1, 0).astype(BF)
-    value = dot(nat, dot(factor_of(weights, 2), quads, 1, 1).astype(BF), 1, 0).astype(BF)
     for part in range(4):
         at = part * TOK
         tok = rows_ref[2 * part * TOK : (2 * part + 1) * TOK, :]
+        left_ref[:, at : at + TOK] = dot(pairs, tok, 1, 1).astype(BF)
         cot_ref[at : at + TOK, :] = rows_ref[(2 * part + 1) * TOK : (2 * part + 2) * TOK, :]
-        left_ref[:, at : at + TOK] = dot(pairs, tok, 1, 1).astype(BF)
-        mixed = dot(recv_ref[:, at : at + TOK], down, 0, 0)
-        out_ref[2 * part * TOK : (2 * part + 1) * TOK, :] = mixed.astype(BF)
-        back = dot(gate, recv_ref[:, SLAB + at : SLAB + at + TOK], 1, 0) + dot(
-            value, recv_ref[:, 2 * SLAB + at : 2 * SLAB + at + TOK], 1, 0
-        )
-        out_ref[(2 * part + 1) * TOK : (2 * part + 2) * TOK, :] = back.T.astype(BF)
     gate_grad = dot(left_ref[...], recv_ref[:, SLAB : 2 * SLAB], 1, 1).astype(BF)
     value_grad = dot(left_ref[...], recv_ref[:, 2 * SLAB :], 1, 1).astype(BF)
     down_grad = dot(recv_ref[:, :SLAB], cot_ref[...], 1, 0)
@@ -176,17 +175,37 @@
         axis=1,
     )
     for half in range(2):
-        take = lambda group: one_hot(
-            (PAIR, PAIR),
-            lambda r, c: (((r >> 2) & 1) == group)
-            & (c == half * WIDTH + (r >> 3) * 4 + (r & 3)),
+        grad_ref[half * PAIR : (half + 1) * PAIR, :] = (
+            dot(owner_rows(half, 0), outer_ref[...], 1, 0) + dot(owner_rows(half, 1), inner, 1, 0)
+        ).astype(BF)
+
+
+def output_kernel(quad_ref, weights_ref, recv_ref, *out_refs):
+    nat = natural_from_pairs()
+    quads = quads_from_natural()
+    weights = weights_ref[...]
+    down = factor_of(weights, 5)
+    gate = dot(nat, dot(factor_of(weights, 0), quads, 1, 1).astype(BF), 1, 0).astype(BF)
+    value = dot(nat, dot(factor_of(weights, 2), quads, 1, 1).astype(BF), 1, 0).astype(BF)
+    quad = quad_ref[0]
+    for hop in range(4):
+        at = pl.multiple_of((quad ^ hop) * TOK, TOK)
+        mixed = dot(recv_ref[:, pl.ds(at, TOK)], down, 0, 0)
+        out_refs[hop][:TOK, :] = mixed.astype(BF)
+        back = dot(gate, recv_ref[:, pl.ds(SLAB + at, TOK)], 1, 0) + dot(
+            value, recv_ref[:, pl.ds(2 * SLAB + at, TOK)], 1, 0
         )
-        grad_ref[half * PAIR : (half + 1) * PAIR, :] = (
-            dot(take(0), outer_ref[...], 1, 0) + dot(take(1), inner, 1, 0)
-        ).astype(BF)
-
-
-def end_kernel(count_z, scale, rows_ref, grads_ref, mixed_ref, back_ref, *grad_refs):
+        out_refs[hop][TOK:, :] = back.T.astype(BF)
+
+
+def place_kernel(quad_ref, own_ref, one_ref, two_ref, three_ref, mixed_ref, back_ref):
+    for hop, ref in enumerate((own_ref, one_ref, two_ref, three_ref)):
+        at = pl.multiple_of((quad_ref[0] ^ hop) * PAIR, PAIR)
+        mixed_ref[:, pl.ds(at, PAIR)] = ref[:TOK, :]
+        back_ref[:, pl.ds(at, PAIR)] = ref[TOK:, :]
+
+
+def end_kernel(count_z, scale, grads_ref, *grad_refs):
     def test(r, c):
         inner = c & 3
         group = (c >> 2) & 1
@@ -202,20 +221,22 @@
                 grad_refs[group * 3 + third][block] = total[
                     row : row + 2, third * WIDTH : (third + 1) * WIDTH
                 ]
-    for part in range(4):
-        cols = slice(part * PAIR, (part + 1) * PAIR)
-        mixed_ref[:, cols] = rows_ref[2 * part * TOK : (2 * part + 1) * TOK, :]
-        back_ref[:, cols] = rows_ref[(2 * part + 1) * TOK : (2 * part + 2) * TOK, :]
-
-
-def call(kernel, name, outs, scratch=()):
+
+
+def call(kernel, name, outs, scratch=(), room=40, **specs):
     return pl.pallas_call(
         kernel,
         out_shape=outs,
         scratch_shapes=list(scratch),
-        compiler_params=pltpu.CompilerParams(vmem_limit_bytes=40 * 1024 * 1024),
+        compiler_params=pltpu.CompilerParams(vmem_limit_bytes=room * 1024 * 1024),
         name=name,
-    )
+        **specs,
+    )
+
+
+def scalar_first(arrays):
+    vmem = pl.BlockSpec(memory_space=pltpu.VMEM)
+    return [pl.BlockSpec(memory_space=pltpu.SMEM)] + [vmem] * arrays
 
 
 def shape(dims, kind=BF):
@@ -229,43 +250,58 @@
     scale = float(tokens.shape[0] * lax.axis_size(DP)) ** (-0.5)
     quad = lax.axis_index(QUAD)
 
-    mine = jnp.concatenate(
-        [gate_inner, gate_outer, value_inner, value_outer, down_inner, down_outer], axis=0
+    rows, mine = call(
+        pack_kernel,
+        "pack",
+        (shape((8 * TOK, PAIR)), shape((48, 2, WIDTH))),
+        room=60,
+    )(
+        tokens,
+        cotangent,
+        gate_inner,
+        gate_outer,
+        value_inner,
+        value_outer,
+        down_inner,
+        down_outer,
     )
     near = lax.all_gather(mine, QUAD, axis=0, tiled=True).reshape(4, 6, 8, 2, WIDTH)
     near = lax.dynamic_slice_in_dim(near, quad * 2, 2, 2)
     near = near.transpose(0, 2, 3, 1, 4).reshape(16, 6 * WIDTH)
-
-    rows = call(split_kernel, "split", shape((8 * TOK, PAIR)))(tokens, cotangent)
+    near, rows = lax.optimization_barrier((near, rows))
     rows = lax.all_to_all(rows, QUAD, split_axis=0, concat_axis=0, tiled=True)
     gathered = lax.all_gather(near, "z", axis=0, tiled=True)
 
+    wide, slab = shape((PAIR, 3 * SLAB)), pltpu.VMEM((PAIR, SLAB), BF)
     send, weights = call(
-        functools.partial(first_kernel, count_z),
-        "first",
-        (shape((PAIR, 3 * SLAB)), shape((PAIR, 6 * WIDTH))),
+        functools.partial(first_kernel, count_z), "first", (wide, shape((PAIR, 6 * WIDTH)))
     )(gathered, rows)
     recv = lax.all_to_all(send, PLANE, split_axis=0, concat_axis=0, tiled=True)
-    send, outer_grads = call(
-        middle_kernel,
-        "middle",
-        (shape((PAIR, 3 * SLAB)), shape((PAIR, 3 * WIDTH))),
-        [pltpu.VMEM((PAIR, SLAB), BF)] * 3,
-    )(weights, recv)
+    send, outer = call(middle_kernel, "middle", (wide, shape((PAIR, 3 * WIDTH))), [slab] * 3)(
+        weights, recv
+    )
     recv = lax.all_to_all(send, PLANE, split_axis=0, concat_axis=0, tiled=True)
-    out_rows, grads = call(
-        last_kernel,
-        "last",
-        (shape((8 * TOK, PAIR)), shape((2 * PAIR, 3 * WIDTH))),
-        [pltpu.VMEM((PAIR, SLAB), BF), pltpu.VMEM((SLAB, PAIR), BF)],
-    )(weights, rows, recv, outer_grads)
-    out_rows = lax.all_to_all(out_rows, QUAD, split_axis=0, concat_axis=0, tiled=True)
+    grads = call(
+        inner_kernel,
+        "inner",
+        shape((2 * PAIR, 3 * WIDTH)),
+        [slab, pltpu.VMEM((SLAB, PAIR), BF)],
+    )(rows, recv, outer)
     grads = lax.all_to_all(grads, DP, split_axis=0, concat_axis=0, tiled=True)
-    mixed, back, g_gate_o, g_value_o, g_down_i, g_gate_i, g_value_i, g_down_o = call(
-        functools.partial(end_kernel, count_z, scale),
-        "end",
-        (shape((TOK, 4 * PAIR)),) * 2 + (shape((8, 2, WIDTH), F32),) * 6,
-    )(out_rows, grads)
+    quad = jnp.reshape(quad, (1,))
+    own, *away = call(
+        output_kernel, "output", (shape((2 * TOK, PAIR)),) * 4, in_specs=scalar_first(2)
+    )(quad, weights, recv)
+    away = [
+        lax.ppermute(part, QUAD, [(at, at ^ hop) for at in range(4)])
+        for hop, part in enumerate(away, 1)
+    ]
+    mixed, back = call(
+        place_kernel, "place", (shape((TOK, 4 * PAIR)),) * 2, in_specs=scalar_first(4)
+    )(quad, own, *away)
+    g_gate_o, g_value_o, g_down_i, g_gate_i, g_value_i, g_down_o = call(
+        functools.partial(end_kernel, count_z, scale), "end", (shape((8, 2, WIDTH), F32),) * 6
+    )(grads)
     return mixed, back, g_gate_i, g_gate_o, g_value_i, g_value_o, g_down_i, g_down_o
 
 

time: 178 us -> 150 us (0.84)
  blocking collectives: 156 us -> 101 us
  waiting for transfers between devices: 0.01 us -> 17 us
  starting transfers between devices: 10.5 us -> 19.4 us
  Pallas kernels: 8.04 us -> 11.3 us
  local copies, waits for them, and re-layouts: 2.21 us -> 0.03 us
    all_to_all x2 -> x0, blocking collectives: 52.1 us -> none  [the longest x1 35.6 us: local(): grads = lax.all_to_all(grads, DP, split_axis=0, concat_axis=0, tiled=True)]
    ppermute x0 -> x3, waiting for transfers between devices: none -> 13.6 us  [local(): lax.ppermute(part, QUAD, [(at, at ^ hop) for at in range(4)])]
    all_to_all x0 -> x1, starting transfers between devices: none -> 7.87 us  [local(): grads = lax.all_to_all(grads, DP, split_axis=0, concat_axis=0, tiled=True)]
    ppermute x0 -> x3, starting transfers between devices: none -> 7.87 us  [local(): lax.ppermute(part, QUAD, [(at, at ^ hop) for at in range(4)])]
    all_to_all x1, starting transfers between devices: 10.5 us -> 3.66 us  [local(): rows = lax.all_to_all(rows, QUAD, split_axis=0, concat_axis=0, tiled=True)]
    all_to_all x0 -> x1, waiting for transfers between devices: none -> 3.39 us  [local(): grads = lax.all_to_all(grads, DP, split_axis=0, concat_axis=0, tiled=True)]
    all_gather x1, blocking collectives: 15.5 us -> 12.2 us  [local(): lax.all_gather(mine, QUAD, axis=0, tiled=True).reshape(4, 6, 8, 2, WIDTH)]
    pallas_call x5 -> x7, Pallas kernels: 8.04 us -> 11.3 us  [the longest x1 2.61 us: local(): call(middle_kernel, 'middle', (wide, shape((PAIR, 3 * WIDTH))), [slab] * 3)]
  transfers between devices with their start and end apart: 1 -> 5, of which waited for: 0 -> 3; matrix products, arithmetic and copies ran while one was open for 0% -> 0% of each run, Pallas kernels for 0% -> 2%
where the time goes in v2:
time: 150 us
  blocking collectives  101 us (67%)
  starting transfers between devices  19.4 us (13%)
  waiting for transfers between devices  17 us (11%)
  Pallas kernels  11.3 us (8%)
    all_to_all x2, blocking collectives, local(): recv = lax.all_to_all(send, PLANE, split_axis=0, concat_axis=0, tiled=True)  63.7 us
    all_gather x1, blocking collectives, local(): gathered = lax.all_gather(near, 'z', axis=0, tiled=True)  25.3 us
    ppermute x3, waiting for transfers between devices, local(): lax.ppermute(part, QUAD, [(at, at ^ hop) for at in range(4)])  13.6 us
    all_gather x1, blocking collectives, local(): lax.all_gather(mine, QUAD, axis=0, tiled=True).reshape(4, 6, 8, 2, WIDTH)  12.2 us
    all_to_all x1, starting transfers between devices, local(): grads = lax.all_to_all(grads, DP, split_axis=0, concat_axis=0, tiled=True)  7.87 us
    ppermute x3, starting transfers between devices, local(): lax.ppermute(part, QUAD, [(at, at ^ hop) for at in range(4)])  7.87 us
    all_to_all x1, starting transfers between devices, local(): rows = lax.all_to_all(rows, QUAD, split_axis=0, concat_axis=0, tiled=True)  3.66 us
    all_to_all x1, waiting for transfers between devices, local(): grads = lax.all_to_all(grads, DP, split_axis=0, concat_axis=0, tiled=True)  3.39 us
  transfers between devices with their start and end apart: 5, of which 3 were waited for; matrix products, arithmetic and copies ran while one was open for 0% of the time, Pallas kernels for 2%

profile of v2, /device:TPU:1, one launch (start us, length us, event | category | flops | bytes accessed | tf_op | source)
XLA Modules:
  0.0 149.7 jit_solution(10041850850548251525)
XLA Ops:
  0.6 2.3 %pack.1 = (bf16[2048,256]{1,0:T(8,128)(2,1)}, bf16[48,2,128]{2,1,0:T(2,128)(2,1)}) custom-call(bf16[256,1024]{1,0:T(8,128)(2,1)} %refs_0_.1, bf16[256,1024]{1,0:T(8,128)(2,1)} %refs_1_.1, bf16[8,2,128]{2,1,0:T(2,128)(2,1)} %refs_2_.1, bf16[8,2,128]{2,1,0:T(2,128)(2,1)} %refs_3_.1, bf16[8,2,128]{2,1,0:T(2,128)(2,1)} %refs_4_.1, bf16[8,2,128]{2,1,0:T(2,128)(2,1)} %refs_5_.1, ...), custom_call_target="tpu_custom_call" | custom-call | tf_op jit(solution)/shard_map/pack/pallas_call | solution.py:253
  2.9 12.2 %all_gather.6 = bf16[192,2,128]{2,1,0:T(2,128)(2,1)S(1)} all-gather(bf16[48,2,128]{2,1,0:T(2,128)(2,1)} %get-tuple-element.28), channel_id=1, replica_groups=mesh['xlo'=2,'z'=16,'core'=2,'xhi'=2,'y'=4] {'xlo','core'}, dimensions={0}, use_global_device_ids=true | all-gather | bytes 122880 | tf_op jit(solution)/shard_map/all_gather | solution.py:268
  15.2 3.7 %all-to-all-start = ((bf16[4,512,256]{2,1,0:T(8,128)(2,1)}), bf16[4,512,256]{2,1,0:T(8,128)(2,1)S(1)}, u32[]{:S(2)}, u32[]{:S(2)}) async-start(bf16[4,512,256]{2,1,0:T(8,128)(2,1)} %bitcast.24), calls=%async_computation | async-start | bytes 2097152 | tf_op jit(solution)/shard_map/all_to_all | solution.py:272
  18.9 25.3 %all_gather.7.weights_ref = bf16[256,768]{1,0:T(8,128)(2,1)S(1)} all-gather(bf16[16,768]{1,0:T(8,128)(2,1)S(1)} %bitcast.27), channel_id=1, replica_groups=mesh['xlo'=2,'z'=16,'core'=2,'xhi'=2,'y'=4] {'z'}, dimensions={0}, use_global_device_ids=true | all-gather | bytes 417792 | tf_op jit(solution)/shard_map/all_gather | solution.py:273
  44.2 0.0 all-to-all-done
  44.2 1.2 first.1
  45.4 37.1 %all_to_all.44 = bf16[32,8,3072]{2,1,0:T(8,128)(2,1)S(1)} all-to-all(bf16[32,8,3072]{2,1,0:T(8,128)(2,1)S(1)} %bitcast.21), channel_id=1, replica_groups=mesh['xlo'=2,'z'=16,'core'=2,'xhi'=2,'y'=4] {'xhi','y','xlo','core'}, dimensions={0} | all-to-all | bytes 3145728 | tf_op jit(solution)/shard_map/all_to_all | solution.py:279
  82.5 2.6 %middle.1 = (bf16[256,3072]{1,0:T(8,128)(2,1)S(1)}, bf16[256,384]{1,0:T(8,128)(2,1)S(1)}) custom-call(bf16[256,768]{1,0:T(8,128)(2,1)S(1)} %get-tuple-element.32.weights_ref, bf16[256,3072]{1,0:T(8,128)(2,1)S(1)} %bitcast.20), custom_call_target="tpu_custom_call" | custom-call | tf_op jit(solution)/shard_map/middle/pallas_call | solution.py:280
  85.1 26.6 %all_to_all.45 = bf16[32,8,3072]{2,1,0:T(8,128)(2,1)S(1)} all-to-all(bf16[32,8,3072]{2,1,0:T(8,128)(2,1)S(1)} %bitcast.22), channel_id=1, replica_groups=mesh['xlo'=2,'z'=16,'core'=2,'xhi'=2,'y'=4] {'xhi','y','xlo','core'}, dimensions={0} | all-to-all | bytes 3145728 | tf_op jit(solution)/shard_map/all_to_all | solution.py:283
  111.8 2.0 %inner.1 = bf16[512,384]{1,0:T(8,128)(2,1)} custom-call(bf16[2048,256]{1,0:T(8,128)(2,1)S(1)} %bitcast.19, bf16[256,3072]{1,0:T(8,128)(2,1)S(1)} %bitcast.16, bf16[256,384]{1,0:T(8,128)(2,1)S(1)} %get-tuple-element.41.outer_ref), custom_call_target="tpu_custom_call" | custom-call | tf_op jit(solution)/shard_map/inner/pallas_call | solution.py:284
  113.8 7.9 %all-to-all-start.3 = ((bf16[64,8,384]{2,1,0:T(8,128)(2,1)}), bf16[64,8,384]{2,1,0:T(8,128)(2,1)S(1)}, u32[]{:S(2)}, u32[]{:S(2)}) async-start(bf16[64,8,384]{2,1,0:T(8,128)(2,1)} %bitcast.9), calls=%async_computation.3 | async-start | bytes 786432 | tf_op jit(solution)/shard_map/all_to_all | solution.py:290
  121.7 1.3 output.1
  123.0 2.4 %collective-permute-start = (bf16[512,256]{1,0:T(8,128)(2,1)S(1)}, bf16[512,256]{1,0:T(8,128)(2,1)S(1)}, u32[]{:S(2)}, u32[]{:S(2)}) collective-permute-start(bf16[512,256]{1,0:T(8,128)(2,1)S(1)} %get-tuple-element.36), channel_id=1, source_target_pairs={{0,8},{8,0},{256,264},{264,256},{1,9},{9,1},{257,265},{265,257},{2... | collective-permute-start | bytes 786440 | tf_op jit(solution)/shard_map/ppermute | solution.py:296
  125.3 3.3 %collective-permute-start.1 = (bf16[512,256]{1,0:T(8,128)(2,1)S(1)}, bf16[512,256]{1,0:T(8,128)(2,1)S(1)}, u32[]{:S(2)}, u32[]{:S(2)}) collective-permute-start(bf16[512,256]{1,0:T(8,128)(2,1)S(1)} %get-tuple-element.37), channel_id=1, source_target_pairs={{0,256},{8,264},{256,0},{264,8},{1,257},{9,265},{257,1},{265,9},{2... | collective-permute-start | bytes 786440 | tf_op jit(solution)/shard_map/ppermute | solution.py:296
  128.6 2.2 %collective-permute-start.2 = (bf16[512,256]{1,0:T(8,128)(2,1)S(1)}, bf16[512,256]{1,0:T(8,128)(2,1)S(1)}, u32[]{:S(2)}, u32[]{:S(2)}) collective-permute-start(bf16[512,256]{1,0:T(8,128)(2,1)S(1)} %get-tuple-element.38), channel_id=1, source_target_pairs={{0,264},{8,256},{256,8},{264,0},{1,265},{9,257},{257,9},{265,1},{2... | collective-permute-start | bytes 786440 | tf_op jit(solution)/shard_map/ppermute | solution.py:296
  130.8 0.0 collective-permute-done.one_ref
  130.9 6.2 %collective-permute-done.1.two_ref = bf16[512,256]{1,0:T(8,128)(2,1)S(1)} collective-permute-done((bf16[512,256]{1,0:T(8,128)(2,1)S(1)}, bf16[512,256]{1,0:T(8,128)(2,1)S(1)}, u32[]{:S(2)}, u32[]{:S(2)}) %collective-permute-start.1) | collective-permute-done | bytes 262176 | tf_op jit(solution)/shard_map/ppermute | solution.py:296
  137.0 7.4 %collective-permute-done.2.three_ref = bf16[512,256]{1,0:T(8,128)(2,1)S(1)} collective-permute-done((bf16[512,256]{1,0:T(8,128)(2,1)S(1)}, bf16[512,256]{1,0:T(8,128)(2,1)S(1)}, u32[]{:S(2)}, u32[]{:S(2)}) %collective-permute-start.2) | collective-permute-done | bytes 262176 | tf_op jit(solution)/shard_map/ppermute | solution.py:296
  144.4 1.1 place.1
  145.5 3.4 %all-to-all-done.3 = bf16[64,8,384]{2,1,0:T(8,128)(2,1)S(1)} async-done(((bf16[64,8,384]{2,1,0:T(8,128)(2,1)}), bf16[64,8,384]{2,1,0:T(8,128)(2,1)S(1)}, u32[]{:S(2)}, u32[]{:S(2)}) %all-to-all-start.3) | async-done | bytes 393248 | tf_op jit(solution)/shard_map/all_to_all | solution.py:290
  148.9 0.8 end.1
  (3 shorter events, 0.0 us)
Async XLA Ops:
  15.2 29.0 %all-to-all-start = ((bf16[4,512,256]{2,1,0:T(8,128)(2,1)}), bf16[4,512,256]{2,1,0:T(8,128)(2,1)S(1)}, u32[]{:S(2)}, u32[]{:S(2)}) async-start(bf16[4,512,256]{2,1,0:T(8,128)(2,1)} %bitcast.24), calls=%async_computation | async-start | bytes 2097152 | tf_op jit(solution)/shard_map/all_to_all | solution.py:272
  113.8 35.1 %all-to-all-start.3 = ((bf16[64,8,384]{2,1,0:T(8,128)(2,1)}), bf16[64,8,384]{2,1,0:T(8,128)(2,1)S(1)}, u32[]{:S(2)}, u32[]{:S(2)}) async-start(bf16[64,8,384]{2,1,0:T(8,128)(2,1)} %bitcast.9), calls=%async_computation.3 | async-start | bytes 786432 | tf_op jit(solution)/shard_map/all_to_all | solution.py:290
  123.0 7.9 %collective-permute-start = (bf16[512,256]{1,0:T(8,128)(2,1)S(1)}, bf16[512,256]{1,0:T(8,128)(2,1)S(1)}, u32[]{:S(2)}, u32[]{:S(2)}) collective-permute-start(bf16[512,256]{1,0:T(8,128)(2,1)S(1)} %get-tuple-element.36), channel_id=1, source_target_pairs={{0,8},{8,0},{256,264},{264,256},{1,9},{9,1},{257,265},{265,257},{2... | collective-permute-start | bytes 786440 | tf_op jit(solution)/shard_map/ppermute | solution.py:296
  125.3 11.7 %collective-permute-start.1 = (bf16[512,256]{1,0:T(8,128)(2,1)S(1)}, bf16[512,256]{1,0:T(8,128)(2,1)S(1)}, u32[]{:S(2)}, u32[]{:S(2)}) collective-permute-start(bf16[512,256]{1,0:T(8,128)(2,1)S(1)} %get-tuple-element.37), channel_id=1, source_target_pairs={{0,256},{8,264},{256,0},{264,8},{1,257},{9,265},{257,1},{265,9},{2... | collective-permute-start | bytes 786440 | tf_op jit(solution)/shard_map/ppermute | solution.py:296
  128.6 15.8 %collective-permute-start.2 = (bf16[512,256]{1,0:T(8,128)(2,1)S(1)}, bf16[512,256]{1,0:T(8,128)(2,1)S(1)}, u32[]{:S(2)}, u32[]{:S(2)}) collective-permute-start(bf16[512,256]{1,0:T(8,128)(2,1)S(1)} %get-tuple-element.38), channel_id=1, source_target_pairs={{0,264},{8,256},{256,8},{264,0},{1,265},{9,257},{257,9},{265,1},{2... | collective-permute-start | bytes 786440 | tf_op jit(solution)/shard_map/ppermute | solution.py:296

commit v3 on v2

v3 whole, which is shorter than its diff:
```python
import functools

import jax
import jax.numpy as jnp
from jax import lax
from jax.experimental import pallas as pl
from jax.experimental.pallas import tpu as pltpu
from jax.sharding import Mesh, PartitionSpec as P

BF = jnp.bfloat16
F32 = jnp.float32
AXES = ("xlo", "z", "core", "xhi", "y")
QUAD = ("xlo", "core")
PLANE = ("xhi", "y", "xlo", "core")
DP = ("xlo", "z", "core")
WIDTH = 128
PAIR = 256
TOK = 256
SLAB = 1024


def dot(left, right, left_dim, right_dim):
    return lax.dot_general(
        left, right, (((left_dim,), (right_dim,)), ((), ())), preferred_element_type=F32
    )


def one_hot(shape, test):
    rows = lax.broadcasted_iota(jnp.int32, shape, 0)
    cols = lax.broadcasted_iota(jnp.int32, shape, 1)
    return jnp.where(test(rows, cols), 1.0, 0.0).astype(BF)


def pairs_from_natural():
    return one_hot(
        (PAIR, PAIR),
        lambda r, c: c == ((r >> 1) & 1) * WIDTH + (r >> 2) * 2 + (r & 1),
    )


def natural_from_pairs():
    return one_hot(
        (PAIR, PAIR),
        lambda r, c: r == ((c >> 1) & 1) * WIDTH + (c >> 2) * 2 + (c & 1),
    )


def quads_from_natural():
    return one_hot(
        (PAIR, PAIR),
        lambda r, c: c == ((r >> 2) & 1) * WIDTH + (r >> 3) * 4 + (r & 3),
    )


def group_rows(group):
    return one_hot((PAIR, 2 * PAIR), lambda r, c: c == (r >> 2) * 8 + group * 4 + (r & 3))


def owner_rows(group):
    return one_hot(
        (2 * PAIR, PAIR),
        lambda r, c: (((r >> 2) & 1) == group) & (c == (r >> 3) * 4 + (r & 3)),
    )


def expand(factor):
    rows = lax.broadcasted_iota(jnp.int32, factor.shape, 0)
    first = ((rows >> 1) & 1) == 0
    zero = jnp.zeros_like(factor)
    return jnp.concatenate(
        [jnp.where(first, factor, zero), jnp.where(first, zero, factor)], axis=1
    )


def own_block(full):
    rows = lax.broadcasted_iota(jnp.int32, (PAIR, WIDTH), 0)
    return jnp.where(((rows >> 1) & 1) == 0, full[:, :WIDTH], full[:, WIDTH:])


def factor_of(rows, index):
    return expand(rows[:, index * WIDTH : (index + 1) * WIDTH])


def share_kernel(count_z, *refs):
    factor_refs, (share_ref, rows_ref, sems) = refs[:6], refs[6:]
    copies = [
        pltpu.make_async_copy(ref, rows_ref.at[at], sems.at[at])
        for at, ref in enumerate(factor_refs)
    ]
    for copy in copies:
        copy.start()
    for copy in copies:
        copy.wait()
    for xlo in range(2):
        thirds = []
        for third in range(3):
            rows = [
                rows_ref[group * 3 + third, (xlo * 2 + core) * 2 + k].astype(F32)
                for core in range(2)
                for group in range(2)
                for k in range(2)
            ]
            thirds.append(jnp.concatenate(rows, axis=0).astype(BF))
        slab = jnp.concatenate(thirds, axis=1)
        for zed in range(count_z):
            at = (xlo * count_z + zed) * 16
            share_ref[at : at + 16, :] = slab


def cut_piece(quad_ref, tok_ref, cot_ref, hop, ref):
    cols = pl.ds(pl.multiple_of((quad_ref[0] ^ hop) * PAIR, PAIR), PAIR)
    ref[:TOK, :] = tok_ref[:, cols]
    ref[TOK:, :] = cot_ref[:, cols]


def far_kernel(quad_ref, tok_ref, cot_ref, two_ref, three_ref):
    cut_piece(quad_ref, tok_ref, cot_ref, 2, two_ref)
    cut_piece(quad_ref, tok_ref, cot_ref, 3, three_ref)


def near_kernel(quad_ref, tok_ref, cot_ref, after_ref, own_ref, one_ref, *order_refs):
    del after_ref
    cut_piece(quad_ref, tok_ref, cot_ref, 0, own_ref)
    cut_piece(quad_ref, tok_ref, cot_ref, 1, one_ref)
    pairs_ref, quads_ref, first_ref, second_ref = order_refs
    pairs_ref[...] = pairs_from_natural()
    quads_ref[...] = quads_from_natural()
    first_ref[...] = owner_rows(0)
    second_ref[...] = owner_rows(1)


def first_kernel(quad_ref, share_ref, *refs):
    piece_refs, (quads_ref, send_ref, weights_ref) = refs[:4], refs[4:]
    share, nat, quads = share_ref[...], natural_from_pairs(), quads_ref[...]
    weights = jnp.concatenate(
        [dot(group_rows(0), share, 1, 0), dot(group_rows(1), share, 1, 0)], axis=1
    ).astype(BF)
    weights_ref[...] = weights
    gate = dot(quads, dot(nat, factor_of(weights, 0), 1, 0).astype(BF), 1, 1).astype(BF)
    value = dot(quads, dot(nat, factor_of(weights, 1), 1, 0).astype(BF), 1, 1).astype(BF)
    down = factor_of(weights, 2)
    for hop, ref in enumerate(piece_refs):
        at = pl.multiple_of((quad_ref[0] ^ hop) * TOK, TOK)
        tok, cot = ref[:TOK, :], ref[TOK:, :]
        send_ref[:, pl.ds(at, TOK)] = dot(gate, tok, 1, 1).astype(BF)
        send_ref[:, pl.ds(SLAB + at, TOK)] = dot(value, tok, 1, 1).astype(BF)
        send_ref[:, pl.ds(2 * SLAB + at, TOK)] = dot(down, cot, 1, 1).astype(BF)


def middle_kernel(
    weights_ref,
    recv_ref,
    pairs_ref,
    quads_ref,
    send_ref,
    grad_ref,
    hid_ref,
    gate_ref,
    value_ref,
):
    pairs, quads = pairs_ref[...], quads_ref[...]
    weights = weights_ref[...]
    gate_w = factor_of(weights, 3)
    value_w = factor_of(weights, 4)
    down_w = factor_of(weights, 5)
    gate_fwd = dot(pairs, gate_w, 1, 1).astype(BF)
    value_fwd = dot(pairs, value_w, 1, 1).astype(BF)
    gate_bwd = dot(gate_w, pairs, 1, 1).astype(BF)
    value_bwd = dot(value_w, pairs, 1, 1).astype(BF)
    down_fwd = dot(quads, down_w, 1, 1).astype(BF)
    down_bwd = dot(down_w, quads, 1, 1).astype(BF)
    gate_pre = dot(gate_fwd, recv_ref[:, :SLAB], 1, 0)
    value_pre = dot(value_fwd, recv_ref[:, SLAB : 2 * SLAB], 1, 0)
    sigma = jax.nn.sigmoid(gate_pre)
    hidden = (gate_pre * sigma * value_pre).astype(BF)
    hid_ref[...] = hidden
    send_ref[:, :SLAB] = dot(down_fwd, hidden, 1, 0).astype(BF)
    back = dot(down_bwd, recv_ref[:, 2 * SLAB :], 1, 0)
    gate_back = (back * value_pre * sigma * (1.0 + gate_pre * (1.0 - sigma))).astype(BF)
    value_back = (back * gate_pre * sigma).astype(BF)
    gate_ref[...] = gate_back
    value_ref[...] = value_back
    send_ref[:, SLAB : 2 * SLAB] = dot(gate_bwd, gate_back, 1, 0).astype(BF)
    send_ref[:, 2 * SLAB :] = dot(value_bwd, value_back, 1, 0).astype(BF)
    gate_grad = dot(recv_ref[:, :SLAB], gate_ref[...], 1, 1).astype(BF)
    value_grad = dot(recv_ref[:, SLAB : 2 * SLAB], value_ref[...], 1, 1).astype(BF)
    down_grad = dot(hid_ref[...], recv_ref[:, 2 * SLAB :], 1, 1).astype(BF)
    grad_ref[:, :WIDTH] = own_block(dot(gate_grad, pairs, 1, 0)).astype(BF)
    grad_ref[:, WIDTH : 2 * WIDTH] = own_block(dot(value_grad, pairs, 1, 0)).astype(BF)
    grad_ref[:, 2 * WIDTH :] = own_block(dot(down_grad, quads, 1, 0)).astype(BF)


def inner_kernel(quad_ref, *refs):
    piece_refs, (recv_ref, outer_ref, pairs_ref, quads_ref, first_ref, second_ref, grad_ref) = (
        refs[:4],
        refs[4:],
    )
    pairs, quads = pairs_ref[...], quads_ref[...]
    gate_grad = value_grad = down_grad = 0.0
    for hop, ref in enumerate(piece_refs):
        at = pl.multiple_of((quad_ref[0] ^ hop) * TOK, TOK)
        tok, cot = ref[:TOK, :], ref[TOK:, :]
        gate_grad += dot(recv_ref[:, pl.ds(SLAB + at, TOK)], tok, 1, 0)
        value_grad += dot(recv_ref[:, pl.ds(2 * SLAB + at, TOK)], tok, 1, 0)
        down_grad += dot(recv_ref[:, pl.ds(at, TOK)], cot, 1, 0)
    gate_grad = dot(pairs, gate_grad.astype(BF), 1, 1).astype(BF)
    value_grad = dot(pairs, value_grad.astype(BF), 1, 1).astype(BF)
    inner = jnp.concatenate(
        [
            own_block(dot(gate_grad, quads, 1, 0)).astype(BF),
            own_block(dot(value_grad, quads, 1, 0)).astype(BF),
            own_block(down_grad).astype(BF),
        ],
        axis=1,
    )
    grad_ref[...] = (
        dot(first_ref[...], outer_ref[...], 1, 0) + dot(second_ref[...], inner, 1, 0)
    ).astype(BF)


def output_kernel(hops, quad_ref, weights_ref, recv_ref, *refs):
    out_refs = refs[-2:]
    nat = natural_from_pairs()
    quads = quads_from_natural()
    weights = weights_ref[...]
    down = factor_of(weights, 2)
    gate = dot(nat, dot(factor_of(weights, 0), quads, 1, 1).astype(BF), 1, 0).astype(BF)
    value = dot(nat, dot(factor_of(weights, 1), quads, 1, 1).astype(BF), 1, 0).astype(BF)
    quad = quad_ref[0]
    for hop, out_ref in zip(hops, out_refs):
        at = pl.multiple_of((quad ^ hop) * TOK, TOK)
        mixed = dot(recv_ref[:, pl.ds(at, TOK)], down, 0, 0)
        out_ref[:TOK, :] = mixed.astype(BF)
        back = dot(gate, recv_ref[:, pl.ds(SLAB + at, TOK)], 1, 0) + dot(
            value, recv_ref[:, pl.ds(2 * SLAB + at, TOK)], 1, 0
        )
        out_ref[TOK:, :] = back.T.astype(BF)


def place_kernel(quad_ref, own_ref, one_ref, two_ref, three_ref, mixed_ref, back_ref):
    for hop, ref in enumerate((own_ref, one_ref, two_ref, three_ref)):
        at = pl.multiple_of((quad_ref[0] ^ hop) * PAIR, PAIR)
        mixed_ref[:, pl.ds(at, PAIR)] = ref[:TOK, :]
        back_ref[:, pl.ds(at, PAIR)] = ref[TOK:, :]


def end_kernel(count_z, scale, grads_ref, *grad_refs):
    def test(r, c):
        inner = c & 3
        group = (c >> 2) & 1
        core = (c >> 3) & 1
        xlo = (c >> 4) // count_z
        return r == group * 16 + xlo * 8 + core * 4 + inner

    total = dot(one_hot((32, 2 * PAIR), test), grads_ref[...], 1, 0) * scale
    for group in range(2):
        for third in range(3):
            for block in range(8):
                row = group * 16 + block * 2
                grad_refs[group * 3 + third][block] = total[
                    row : row + 2, third * WIDTH : (third + 1) * WIDTH
                ]


def call(kernel, name, outs, scratch=(), room=40, **specs):
    return pl.pallas_call(
        kernel,
        out_shape=outs,
        scratch_shapes=list(scratch),
        compiler_params=pltpu.CompilerParams(vmem_limit_bytes=room * 1024 * 1024),
        name=name,
        **specs,
    )


def scalar_first(arrays):
    vmem = pl.BlockSpec(memory_space=pltpu.VMEM)
    return [pl.BlockSpec(memory_space=pltpu.SMEM)] + [vmem] * arrays


def swap(part, hop):
    return lax.ppermute(part, QUAD, [(at, at ^ hop) for at in range(4)])


def shape(dims, kind=BF):
    return jax.ShapeDtypeStruct(dims, kind)


def local(
    tokens, cotangent, gate_inner, gate_outer, value_inner, value_outer, down_inner, down_outer
):
    count_z = lax.axis_size("z")
    scale = float(tokens.shape[0] * lax.axis_size(DP)) ** (-0.5)

    quad = jnp.reshape(lax.axis_index(QUAD), (1,))
    piece, share = shape((2 * TOK, PAIR)), shape((2 * PAIR, 3 * WIDTH))
    shares = call(
        functools.partial(share_kernel, count_z),
        "share",
        share,
        [pltpu.VMEM((6, 8, 2, WIDTH), BF), pltpu.SemaphoreType.DMA((6,))],
        room=60,
        in_specs=[pl.BlockSpec(memory_space=pl.ANY)] * 6,
    )(gate_inner, value_inner, down_outer, gate_outer, value_outer, down_inner)
    shares = lax.all_to_all(shares, DP, split_axis=0, concat_axis=0, tiled=True)
    two, three = call(far_kernel, "far", (piece,) * 2, room=60, in_specs=scalar_first(2))(
        quad, tokens, cotangent
    )
    square, tall = shape((PAIR, PAIR)), shape((2 * PAIR, PAIR))
    after = [pl.BlockSpec(memory_space=pl.ANY)]
    own, one, pairs, quads, *owners = call(
        near_kernel,
        "near",
        (piece, piece, square, square, tall, tall),
        in_specs=scalar_first(2) + after,
    )(quad, tokens, cotangent, two)
    pieces = (own, swap(one, 1), swap(two, 2), swap(three, 3))

    wide, slab = shape((PAIR, 3 * SLAB)), pltpu.VMEM((PAIR, SLAB), BF)
    send, weights = call(
        first_kernel, "first", (wide, shape((PAIR, 6 * WIDTH))), in_specs=scalar_first(6)
    )(quad, shares, *pieces, quads)
    recv = lax.all_to_all(send, PLANE, split_axis=0, concat_axis=0, tiled=True)
    send, outer = call(middle_kernel, "middle", (wide, shape((PAIR, 3 * WIDTH))), [slab] * 3)(
        weights, recv, pairs, quads
    )
    recv = lax.all_to_all(send, PLANE, split_axis=0, concat_axis=0, tiled=True)
    grads = call(inner_kernel, "inner", share, in_specs=scalar_first(10))(
        quad, *pieces, recv, outer, pairs, quads, *owners
    )
    grads = lax.all_to_all(grads, DP, split_axis=0, concat_axis=0, tiled=True)
    two, three = call(
        functools.partial(output_kernel, (2, 3)), "output", (piece,) * 2, in_specs=scalar_first(2)
    )(quad, weights, recv)
    three = swap(three, 3)
    own, one = call(
        functools.partial(output_kernel, (0, 1)),
        "output2",
        (piece,) * 2,
        in_specs=scalar_first(2) + after,
    )(quad, weights, recv, three)
    mixed, back = call(
        place_kernel, "place", (shape((TOK, 4 * PAIR)),) * 2, in_specs=scalar_first(4)
    )(quad, own, swap(one, 1), swap(two, 2), three)
    g_gate_o, g_value_o, g_down_i, g_gate_i, g_value_i, g_down_o = call(
        functools.partial(end_kernel, count_z, scale), "end", (shape((8, 2, WIDTH), F32),) * 6
    )(grads)
    return mixed, back, g_gate_i, g_gate_o, g_value_i, g_value_o, g_down_i, g_down_o


def solution(mesh):
    fine = Mesh(mesh.devices.reshape(2, 16, 2, 2, 4), AXES)
    rows = P(DP, ("xhi", "y"))
    factor = P(("xhi", "y"), DP, None)
    return jax.shard_map(
        local,
        mesh=fine,
        in_specs=(rows,) * 2 + (factor,) * 6,
        out_specs=(rows,) * 2 + (factor,) * 6,
        check_vma=False,
    )
```

time: 150 us -> 145 us (0.967)
  blocking collectives: 101 us -> 56.2 us
  starting transfers between devices: 19.4 us -> 40.4 us
  waiting for transfers between devices: 17 us -> 31.8 us
  Pallas kernels: 11.3 us -> 13.8 us
  local copies, waits for them, and re-layouts: 0.03 us -> 1.68 us
    all_gather x2 -> x0, blocking collectives: 37.6 us -> none  [the longest x1 25.3 us: local(): gathered = lax.all_gather(near, 'z', axis=0, tiled=True)]
    all_to_all x1, starting transfers between devices: 3.66 us -> 18.1 us  [local(): shares = lax.all_to_all(shares, DP, split_axis=0, concat_axis=0, tiled=True)]
    all_to_all x2, blocking collectives: 63.7 us -> 56.2 us  [local(): recv = lax.all_to_all(send, PLANE, split_axis=0, concat_axis=0, tiled=True)]
    ppermute x3 -> x6, starting transfers between devices: 7.87 us -> 15.4 us  [swap(): return lax.ppermute(part, QUAD, [(at, at ^ hop) for at in range(4)])]
    ppermute x3 -> x6, waiting for transfers between devices: 13.6 us -> 20.6 us  [swap(): return lax.ppermute(part, QUAD, [(at, at ^ hop) for at in range(4)])]
    all_to_all x1, waiting for transfers between devices: 0.01 us -> 5.49 us  [local(): shares = lax.all_to_all(shares, DP, split_axis=0, concat_axis=0, tiled=True)]
    pallas_call x4 -> x7, Pallas kernels: 6.76 us -> 9.64 us  [the longest x1 2.19 us: local(): call(inner_kernel, 'inner', share, in_specs=scalar_first(10))]
    all_to_all x1, waiting for transfers between devices: 3.39 us -> 5.69 us  [local(): grads = lax.all_to_all(grads, DP, split_axis=0, concat_axis=0, tiled=True)]
  transfers between devices with their start and end apart: 5 -> 8, of which waited for: 3 -> 6; matrix products, arithmetic and copies ran while one was open for 0% -> 0% of each run, Pallas kernels for 2% -> 4%
where the time goes in v3:
time: 145 us
  blocking collectives  56.2 us (39%)
  starting transfers between devices  40.4 us (28%)
  waiting for transfers between devices  31.8 us (22%)
  Pallas kernels  13.8 us (10%)
  local copies, waits for them, and re-layouts  1.68 us (1%)
    all_to_all x2, blocking collectives, local(): recv = lax.all_to_all(send, PLANE, split_axis=0, concat_axis=0, tiled=True)  56.2 us
    ppermute x6, waiting for transfers between devices, swap(): return lax.ppermute(part, QUAD, [(at, at ^ hop) for at in range(4)])  20.6 us
    all_to_all x1, starting transfers between devices, local(): shares = lax.all_to_all(shares, DP, split_axis=0, concat_axis=0, tiled=True)  18.1 us
    ppermute x6, starting transfers between devices, swap(): return lax.ppermute(part, QUAD, [(at, at ^ hop) for at in range(4)])  15.4 us
    all_to_all x1, starting transfers between devices, local(): grads = lax.all_to_all(grads, DP, split_axis=0, concat_axis=0, tiled=True)  6.9 us
    all_to_all x1, waiting for transfers between devices, local(): grads = lax.all_to_all(grads, DP, split_axis=0, concat_axis=0, tiled=True)  5.69 us
    all_to_all x1, waiting for transfers between devices, local(): shares = lax.all_to_all(shares, DP, split_axis=0, concat_axis=0, tiled=True)  5.49 us
  transfers between devices with their start and end apart: 8, of which 6 were waited for; matrix products, arithmetic and copies ran while one was open for 0% of the time, Pallas kernels for 4%

profile of v3, /device:TPU:1, one launch (start us, length us, event | category | flops | bytes accessed | tf_op | source)
XLA Modules:
  0.0 144.5 jit_solution(1039250637708598831)
XLA Ops:
  0.6 0.0 copy-start.1
  0.6 0.0 copy-start
  0.7 1.7 %share.1 = bf16[512,384]{1,0:T(8,128)(2,1)} custom-call(bf16[8,2,128]{2,1,0:T(2,128)(2,1)} %refs_0_.1, bf16[8,2,128]{2,1,0:T(2,128)(2,1)} %refs_1_.1, bf16[8,2,128]{2,1,0:T(2,128)(2,1)} %refs_2_.1, bf16[8,2,128]{2,1,0:T(2,128)(2,1)} %refs_3_.1, bf16[8,2,128]{2,1,0:T(2,128)(2,1)} %refs_4_.1, bf16[8,2,128]{2,1,0:T(2,128)(2,1)} %refs_5_.1), custom_call_target="tpu_custom_call" | custom-call | tf_op jit(solution)/shard_map/share/pallas_call | solution.py:297
  2.4 18.1 %all-to-all-start = ((bf16[64,8,384]{2,1,0:T(8,128)(2,1)}), bf16[64,8,384]{2,1,0:T(8,128)(2,1)S(1)}, u32[]{:S(2)}, u32[]{:S(2)}) async-start(bf16[64,8,384]{2,1,0:T(8,128)(2,1)} %bitcast.17), calls=%async_computation | async-start | bytes 786432 | tf_op jit(solution)/shard_map/all_to_all | solution.py:305
  20.5 2.1 %far.1 = (bf16[512,256]{1,0:T(8,128)(2,1)}, bf16[512,256]{1,0:T(8,128)(2,1)}) custom-call(s32[1]{0:T(128)} %bitcast.quad_ref, bf16[256,1024]{1,0:T(8,128)(2,1)} %tok_ref.3, bf16[256,1024]{1,0:T(8,128)(2,1)} %cot_ref.3), custom_call_target="tpu_custom_call" | custom-call | tf_op jit(solution)/shard_map/far/pallas_call | solution.py:306
  22.5 3.6 %collective-permute-start.2 = (bf16[512,256]{1,0:T(8,128)(2,1)}, bf16[512,256]{1,0:T(8,128)(2,1)S(1)}, u32[]{:S(2)}, u32[]{:S(2)}) collective-permute-start(bf16[512,256]{1,0:T(8,128)(2,1)} %get-tuple-element.35), channel_id=1, source_target_pairs={{0,264},{8,256},{256,8},{264,0},{1,265},{9,257},{257,9},{265,1},{2... | collective-permute-start | bytes 786440 | tf_op jit(solution)/shard_map/ppermute | solution.py:282
  26.2 2.0 %collective-permute-start.1 = (bf16[512,256]{1,0:T(8,128)(2,1)}, bf16[512,256]{1,0:T(8,128)(2,1)S(1)}, u32[]{:S(2)}, u32[]{:S(2)}) collective-permute-start(bf16[512,256]{1,0:T(8,128)(2,1)} %get-tuple-element.32.after_ref), channel_id=1, source_target_pairs={{0,256},{8,264},{256,0},{264,8},{1,257},{9,265},{257,1},{265,9},{2... | collective-permute-start | bytes 786440 | tf_op jit(solution)/shard_map/ppermute | solution.py:282
  28.2 0.0 copy-start.4
  28.2 1.0 copy-done.4
  29.1 0.3 near.1
  29.5 0.7 copy-done.2
  30.2 2.2 %collective-permute-start = (bf16[512,256]{1,0:T(8,128)(2,1)S(1)}, bf16[512,256]{1,0:T(8,128)(2,1)S(1)}, u32[]{:S(2)}, u32[]{:S(2)}) collective-permute-start(bf16[512,256]{1,0:T(8,128)(2,1)S(1)} %get-tuple-element.34), channel_id=1, source_target_pairs={{0,8},{8,0},{256,264},{264,256},{1,9},{9,1},{257,265},{265,257},{2... | collective-permute-start | bytes 786440 | tf_op jit(solution)/shard_map/ppermute | solution.py:282
  32.4 2.9 %collective-permute-done.2.refs_3_ = bf16[512,256]{1,0:T(8,128)(2,1)S(1)} collective-permute-done((bf16[512,256]{1,0:T(8,128)(2,1)}, bf16[512,256]{1,0:T(8,128)(2,1)S(1)}, u32[]{:S(2)}, u32[]{:S(2)}) %collective-permute-start.2) | collective-permute-done | bytes 262176 | tf_op jit(solution)/shard_map/ppermute | solution.py:282
  35.3 6.9 %collective-permute-done.1.refs_2_ = bf16[512,256]{1,0:T(8,128)(2,1)S(1)} collective-permute-done((bf16[512,256]{1,0:T(8,128)(2,1)}, bf16[512,256]{1,0:T(8,128)(2,1)S(1)}, u32[]{:S(2)}, u32[]{:S(2)}) %collective-permute-start.1) | collective-permute-done | bytes 262176 | tf_op jit(solution)/shard_map/ppermute | solution.py:282
  42.2 0.0 collective-permute-done.refs_1_
  42.2 5.5 %all-to-all-done = bf16[64,8,384]{2,1,0:T(8,128)(2,1)S(1)} async-done(((bf16[64,8,384]{2,1,0:T(8,128)(2,1)}), bf16[64,8,384]{2,1,0:T(8,128)(2,1)S(1)}, u32[]{:S(2)}, u32[]{:S(2)}) %all-to-all-start) | async-done | bytes 393248 | tf_op jit(solution)/shard_map/all_to_all | solution.py:305
  47.7 1.3 first.1
  49.0 29.4 %all_to_all.44 = bf16[32,8,3072]{2,1,0:T(8,128)(2,1)S(1)} all-to-all(bf16[32,8,3072]{2,1,0:T(8,128)(2,1)S(1)} %bitcast.13), channel_id=1, replica_groups=mesh['xlo'=2,'z'=16,'core'=2,'xhi'=2,'y'=4] {'xhi','y','xlo','core'}, dimensions={0} | all-to-all | bytes 3145728 | tf_op jit(solution)/shard_map/all_to_all | solution.py:323
  78.4 2.2 %middle.1 = (bf16[256,3072]{1,0:T(8,128)(2,1)S(1)}, bf16[256,384]{1,0:T(8,128)(2,1)S(1)}) custom-call(bf16[256,768]{1,0:T(8,128)(2,1)S(1)} %get-tuple-element.37.weights_ref, bf16[256,3072]{1,0:T(8,128)(2,1)S(1)} %bitcast.12, bf16[256,256]{1,0:T(8,128)(2,1)S(1)} %get-tuple-element.39.pairs_ref.refs_6_, ...), custom_call_target="tpu_custom_call" | custom-call | tf_op jit(solution)/shard_map/middle/pallas_call | solution.py:324
  80.7 26.7 %all_to_all.45 = bf16[32,8,3072]{2,1,0:T(8,128)(2,1)S(1)} all-to-all(bf16[32,8,3072]{2,1,0:T(8,128)(2,1)S(1)} %bitcast.14), channel_id=1, replica_groups=mesh['xlo'=2,'z'=16,'core'=2,'xhi'=2,'y'=4] {'xhi','y','xlo','core'}, dimensions={0} | all-to-all | bytes 3145728 | tf_op jit(solution)/shard_map/all_to_all | solution.py:327
  107.4 2.2 %inner.1 = bf16[512,384]{1,0:T(8,128)(2,1)} custom-call(s32[1]{0:T(128)} %bitcast.quad_ref, bf16[512,256]{1,0:T(8,128)(2,1)S(1)} %get-tuple-element.33.refs_0_, bf16[512,256]{1,0:T(8,128)(2,1)S(1)} %collective-permute-done.refs_1_, bf16[512,256]{1,0:T(8,128)(2,1)S(1)} %collective-permute-done.1.refs_2_, bf16[512,256]{1,0:T(8,128)(2,1)S(1)} %collective-permute-done.2.refs_3_, ...), custom_call_target="tpu_custom_call" | custom-call | tf_op jit(solution)/shard_map/inner/pallas_call | solution.py:328
  109.6 6.9 %all-to-all-start.3 = ((bf16[64,8,384]{2,1,0:T(8,128)(2,1)}), bf16[64,8,384]{2,1,0:T(8,128)(2,1)S(1)}, u32[]{:S(2)}, u32[]{:S(2)}) async-start(bf16[64,8,384]{2,1,0:T(8,128)(2,1)} %bitcast.7), calls=%async_computation.3 | async-start | bytes 786432 | tf_op jit(solution)/shard_map/all_to_all | solution.py:331
  116.5 1.1 output.1
  117.5 3.6 %collective-permute-start.3 = (bf16[512,256]{1,0:T(8,128)(2,1)S(1)}, bf16[512,256]{1,0:T(8,128)(2,1)S(1)}, u32[]{:S(2)}, u32[]{:S(2)}) collective-permute-start(bf16[512,256]{1,0:T(8,128)(2,1)S(1)} %get-tuple-element.41), channel_id=1, source_target_pairs={{0,264},{8,256},{256,8},{264,0},{1,265},{9,257},{257,9},{265,1},{2... | collective-permute-start | bytes 786440 | tf_op jit(solution)/shard_map/ppermute | solution.py:282
  121.2 2.0 %collective-permute-start.5 = (bf16[512,256]{1,0:T(8,128)(2,1)S(1)}, bf16[512,256]{1,0:T(8,128)(2,1)S(1)}, u32[]{:S(2)}, u32[]{:S(2)}) collective-permute-start(bf16[512,256]{1,0:T(8,128)(2,1)S(1)} %get-tuple-element.44), channel_id=1, source_target_pairs={{0,256},{8,264},{256,0},{264,8},{1,257},{9,265},{257,1},{265,9},{2... | collective-permute-start | bytes 786440 | tf_op jit(solution)/shard_map/ppermute | solution.py:282
  123.2 6.9 %collective-permute-done.3.refs_0_.three_ref = bf16[512,256]{1,0:T(8,128)(2,1)S(1)} collective-permute-done((bf16[512,256]{1,0:T(8,128)(2,1)S(1)}, bf16[512,256]{1,0:T(8,128)(2,1)S(1)}, u32[]{:S(2)}, u32[]{:S(2)}) %collective-permute-start.3) | collective-permute-done | bytes 262176 | tf_op jit(solution)/shard_map/ppermute | solution.py:282
  130.1 1.0 output2.1
  131.2 1.9 %collective-permute-start.4 = (bf16[512,256]{1,0:T(8,128)(2,1)S(1)}, bf16[512,256]{1,0:T(8,128)(2,1)S(1)}, u32[]{:S(2)}, u32[]{:S(2)}) collective-permute-start(bf16[512,256]{1,0:T(8,128)(2,1)S(1)} %get-tuple-element.43), channel_id=1, source_target_pairs={{0,8},{8,0},{256,264},{264,256},{1,9},{9,1},{257,265},{265,257},{2... | collective-permute-start | bytes 786440 | tf_op jit(solution)/shard_map/ppermute | solution.py:282
  133.1 3.8 %collective-permute-done.5.two_ref = bf16[512,256]{1,0:T(8,128)(2,1)S(1)} collective-permute-done((bf16[512,256]{1,0:T(8,128)(2,1)S(1)}, bf16[512,256]{1,0:T(8,128)(2,1)S(1)}, u32[]{:S(2)}, u32[]{:S(2)}) %collective-permute-start.5) | collective-permute-done | bytes 262176 | tf_op jit(solution)/shard_map/ppermute | solution.py:282
  136.9 1.1 place.1
  138.0 5.7 %all-to-all-done.3 = bf16[64,8,384]{2,1,0:T(8,128)(2,1)S(1)} async-done(((bf16[64,8,384]{2,1,0:T(8,128)(2,1)}), bf16[64,8,384]{2,1,0:T(8,128)(2,1)S(1)}, u32[]{:S(2)}, u32[]{:S(2)}) %all-to-all-start.3) | async-done | bytes 393248 | tf_op jit(solution)/shard_map/all_to_all | solution.py:331
  143.7 0.8 end.1
  (6 shorter events, 0.0 us)
Async XLA Ops:
  0.6 27.5 %copy-start.1 = (bf16[256,1024]{1,0:T(8,128)(2,1)S(1)}, bf16[256,1024]{1,0:T(8,128)(2,1)}, u32[]{:S(2)}) copy-start(bf16[256,1024]{1,0:T(8,128)(2,1)} %cot_ref.3) | copy-start | bytes 1572868
  0.6 27.5 %copy-start = (bf16[256,1024]{1,0:T(8,128)(2,1)S(1)}, bf16[256,1024]{1,0:T(8,128)(2,1)}, u32[]{:S(2)}) copy-start(bf16[256,1024]{1,0:T(8,128)(2,1)} %tok_ref.3) | copy-start | bytes 1572868
  2.4 45.3 %all-to-all-start = ((bf16[64,8,384]{2,1,0:T(8,128)(2,1)}), bf16[64,8,384]{2,1,0:T(8,128)(2,1)S(1)}, u32[]{:S(2)}, u32[]{:S(2)}) async-start(bf16[64,8,384]{2,1,0:T(8,128)(2,1)} %bitcast.17), calls=%async_computation | async-start | bytes 786432 | tf_op jit(solution)/shard_map/all_to_all | solution.py:305
  22.5 12.8 %collective-permute-start.2 = (bf16[512,256]{1,0:T(8,128)(2,1)}, bf16[512,256]{1,0:T(8,128)(2,1)S(1)}, u32[]{:S(2)}, u32[]{:S(2)}) collective-permute-start(bf16[512,256]{1,0:T(8,128)(2,1)} %get-tuple-element.35), channel_id=1, source_target_pairs={{0,264},{8,256},{256,8},{264,0},{1,265},{9,257},{257,9},{265,1},{2... | collective-permute-start | bytes 786440 | tf_op jit(solution)/shard_map/ppermute | solution.py:282
  26.2 16.1 %collective-permute-start.1 = (bf16[512,256]{1,0:T(8,128)(2,1)}, bf16[512,256]{1,0:T(8,128)(2,1)S(1)}, u32[]{:S(2)}, u32[]{:S(2)}) collective-permute-start(bf16[512,256]{1,0:T(8,128)(2,1)} %get-tuple-element.32.after_ref), channel_id=1, source_target_pairs={{0,256},{8,264},{256,0},{264,8},{1,257},{9,265},{257,1},{265,9},{2... | collective-permute-start | bytes 786440 | tf_op jit(solution)/shard_map/ppermute | solution.py:282
  28.2 1.0 copy-start.4
  29.5 0.7 copy-start.2
  30.2 12.0 %collective-permute-start = (bf16[512,256]{1,0:T(8,128)(2,1)S(1)}, bf16[512,256]{1,0:T(8,128)(2,1)S(1)}, u32[]{:S(2)}, u32[]{:S(2)}) collective-permute-start(bf16[512,256]{1,0:T(8,128)(2,1)S(1)} %get-tuple-element.34), channel_id=1, source_target_pairs={{0,8},{8,0},{256,264},{264,256},{1,9},{9,1},{257,265},{265,257},{2... | collective-permute-start | bytes 786440 | tf_op jit(solution)/shard_map/ppermute | solution.py:282
  80.6 26.8 %copy-start.3 = (bf16[512,256]{1,0:T(8,128)(2,1)S(1)}, bf16[512,256]{1,0:T(8,128)(2,1)}, u32[]{:S(2)}) copy-start(bf16[512,256]{1,0:T(8,128)(2,1)} %copy-done.2) | copy-start | bytes 786436
  109.6 34.2 %all-to-all-start.3 = ((bf16[64,8,384]{2,1,0:T(8,128)(2,1)}), bf16[64,8,384]{2,1,0:T(8,128)(2,1)S(1)}, u32[]{:S(2)}, u32[]{:S(2)}) async-start(bf16[64,8,384]{2,1,0:T(8,128)(2,1)} %bitcast.7), calls=%async_computation.3 | async-start | bytes 786432 | tf_op jit(solution)/shard_map/all_to_all | solution.py:331
  117.5 12.6 %collective-permute-start.3 = (bf16[512,256]{1,0:T(8,128)(2,1)S(1)}, bf16[512,256]{1,0:T(8,128)(2,1)S(1)}, u32[]{:S(2)}, u32[]{:S(2)}) collective-permute-start(bf16[512,256]{1,0:T(8,128)(2,1)S(1)} %get-tuple-element.41), channel_id=1, source_target_pairs={{0,264},{8,256},{256,8},{264,0},{1,265},{9,257},{257,9},{265,1},{2... | collective-permute-start | bytes 786440 | tf_op jit(solution)/shard_map/ppermute | solution.py:282
  121.2 15.7 %collective-permute-start.5 = (bf16[512,256]{1,0:T(8,128)(2,1)S(1)}, bf16[512,256]{1,0:T(8,128)(2,1)S(1)}, u32[]{:S(2)}, u32[]{:S(2)}) collective-permute-start(bf16[512,256]{1,0:T(8,128)(2,1)S(1)} %get-tuple-element.44), channel_id=1, source_target_pairs={{0,256},{8,264},{256,0},{264,8},{1,257},{9,265},{257,1},{265,9},{2... | collective-permute-start | bytes 786440 | tf_op jit(solution)/shard_map/ppermute | solution.py:282
  131.2 5.8 %collective-permute-start.4 = (bf16[512,256]{1,0:T(8,128)(2,1)S(1)}, bf16[512,256]{1,0:T(8,128)(2,1)S(1)}, u32[]{:S(2)}, u32[]{:S(2)}) collective-permute-start(bf16[512,256]{1,0:T(8,128)(2,1)S(1)} %get-tuple-element.43), channel_id=1, source_target_pairs={{0,8},{8,0},{256,264},{264,256},{1,9},{9,1},{257,265},{265,257},{2... | collective-permute-start | bytes 786440 | tf_op jit(solution)/shard_map/ppermute | solution.py:282

commit v4 on v3

--- a/solution.py
+++ b/solution.py
@@ -17,6 +17,7 @@
 PAIR = 256
 TOK = 256
 SLAB = 1024
+STEP = 9
 
 
 def dot(left, right, left_dim, right_dim):
@@ -52,14 +53,29 @@
     )
 
 
+def device_at(place):
+    return place >> 5, (((place >> 1) & 15) * STEP) & 15, place & 1
+
+
+def place_of(device):
+    return (device >> 5) * 32 + (((device >> 1) & 15) * STEP & 15) * 2 + (device & 1)
+
+
+def device_index(place):
+    xlo, zed, core = device_at(place)
+    return xlo * 32 + zed * 2 + core
+
+
 def group_rows(group):
-    return one_hot((PAIR, 2 * PAIR), lambda r, c: c == (r >> 2) * 8 + group * 4 + (r & 3))
+    return one_hot(
+        (PAIR, 2 * PAIR), lambda r, c: c == place_of(r >> 2) * 8 + group * 4 + (r & 3)
+    )
 
 
 def owner_rows(group):
     return one_hot(
         (2 * PAIR, PAIR),
-        lambda r, c: (((r >> 2) & 1) == group) & (c == (r >> 3) * 4 + (r & 3)),
+        lambda r, c: (((r >> 2) & 1) == group) & (c == device_index(r >> 3) * 4 + (r & 3)),
     )
 
 
@@ -81,7 +97,7 @@
     return expand(rows[:, index * WIDTH : (index + 1) * WIDTH])
 
 
-def share_kernel(count_z, *refs):
+def share_kernel(*refs):
     factor_refs, (share_ref, rows_ref, sems) = refs[:6], refs[6:]
     copies = [
         pltpu.make_async_copy(ref, rows_ref.at[at], sems.at[at])
@@ -91,20 +107,21 @@
         copy.start()
     for copy in copies:
         copy.wait()
-    for xlo in range(2):
-        thirds = []
-        for third in range(3):
-            rows = [
-                rows_ref[group * 3 + third, (xlo * 2 + core) * 2 + k].astype(F32)
-                for core in range(2)
-                for group in range(2)
-                for k in range(2)
-            ]
-            thirds.append(jnp.concatenate(rows, axis=0).astype(BF))
-        slab = jnp.concatenate(thirds, axis=1)
-        for zed in range(count_z):
-            at = (xlo * count_z + zed) * 16
-            share_ref[at : at + 16, :] = slab
+    slabs = {}
+    for place in range(0, 64, 2):
+        quads = tuple(device_at(at)[0] * 2 + device_at(at)[2] for at in (place, place + 1))
+        if quads not in slabs:
+            thirds = []
+            for third in range(3):
+                rows = [
+                    rows_ref[group * 3 + third, quad * 2 + k].astype(F32)
+                    for quad in quads
+                    for group in range(2)
+                    for k in range(2)
+                ]
+                thirds.append(jnp.concatenate(rows, axis=0).astype(BF))
+            slabs[quads] = jnp.concatenate(thirds, axis=1)
+        share_ref[place * 8 : place * 8 + 16, :] = slabs[quads]
 
 
 def cut_piece(quad_ref, tok_ref, cot_ref, hop, ref):
@@ -244,13 +261,10 @@
         back_ref[:, pl.ds(at, PAIR)] = ref[TOK:, :]
 
 
-def end_kernel(count_z, scale, grads_ref, *grad_refs):
+def end_kernel(scale, grads_ref, *grad_refs):
     def test(r, c):
-        inner = c & 3
-        group = (c >> 2) & 1
-        core = (c >> 3) & 1
-        xlo = (c >> 4) // count_z
-        return r == group * 16 + xlo * 8 + core * 4 + inner
+        xlo, _, core = device_at(c >> 3)
+        return r == ((c >> 2) & 1) * 16 + xlo * 8 + core * 4 + (c & 3)
 
     total = dot(one_hot((32, 2 * PAIR), test), grads_ref[...], 1, 0) * scale
     for group in range(2):
@@ -278,6 +292,13 @@
     return [pl.BlockSpec(memory_space=pltpu.SMEM)] + [vmem] * arrays
 
 
+def exchange(rows):
+    order = [[device_index(place) for place in range(64)]]
+    return lax.all_to_all(
+        rows, DP, split_axis=0, concat_axis=0, axis_index_groups=order, tiled=True
+    )
+
+
 def swap(part, hop):
     return lax.ppermute(part, QUAD, [(at, at ^ hop) for at in range(4)])
 
@@ -289,20 +310,19 @@
 def local(
     tokens, cotangent, gate_inner, gate_outer, value_inner, value_outer, down_inner, down_outer
 ):
-    count_z = lax.axis_size("z")
     scale = float(tokens.shape[0] * lax.axis_size(DP)) ** (-0.5)
 
     quad = jnp.reshape(lax.axis_index(QUAD), (1,))
     piece, share = shape((2 * TOK, PAIR)), shape((2 * PAIR, 3 * WIDTH))
     shares = call(
-        functools.partial(share_kernel, count_z),
+        share_kernel,
         "share",
         share,
         [pltpu.VMEM((6, 8, 2, WIDTH), BF), pltpu.SemaphoreType.DMA((6,))],
         room=60,
         in_specs=[pl.BlockSpec(memory_space=pl.ANY)] * 6,
     )(gate_inner, value_inner, down_outer, gate_outer, value_outer, down_inner)
-    shares = lax.all_to_all(shares, DP, split_axis=0, concat_axis=0, tiled=True)
+    shares = exchange(shares)
     two, three = call(far_kernel, "far", (piece,) * 2, room=60, in_specs=scalar_first(2))(
         quad, tokens, cotangent
     )
@@ -328,7 +348,7 @@
     grads = call(inner_kernel, "inner", share, in_specs=scalar_first(10))(
         quad, *pieces, recv, outer, pairs, quads, *owners
     )
-    grads = lax.all_to_all(grads, DP, split_axis=0, concat_axis=0, tiled=True)
+    grads = exchange(grads)
     two, three = call(
         functools.partial(output_kernel, (2, 3)), "output", (piece,) * 2, in_specs=scalar_first(2)
     )(quad, weights, recv)
@@ -343,7 +363,7 @@
         place_kernel, "place", (shape((TOK, 4 * PAIR)),) * 2, in_specs=scalar_first(4)
     )(quad, own, swap(one, 1), swap(two, 2), three)
     g_gate_o, g_value_o, g_down_i, g_gate_i, g_value_i, g_down_o = call(
-        functools.partial(end_kernel, count_z, scale), "end", (shape((8, 2, WIDTH), F32),) * 6
+        functools.partial(end_kernel, scale), "end", (shape((8, 2, WIDTH), F32),) * 6
     )(grads)
     return mixed, back, g_gate_i, g_gate_o, g_value_i, g_value_o, g_down_i, g_down_o
 

time: 145 us -> 143 us (0.986)
  waiting for transfers between devices: 31.8 us -> 27.5 us
  starting transfers between devices: 40.4 us -> 42.4 us
    all_to_all x2, waiting for transfers between devices: 11.2 us -> 7.64 us  [exchange(): lax.all_to_all(rows, DP, split_axis=0, concat_axis=0, axis_index_groups=o...]
    all_to_all x2, starting transfers between devices: 25 us -> 27 us  [exchange(): lax.all_to_all(rows, DP, split_axis=0, concat_axis=0, axis_index_groups=o...]
where the time goes in v4:
time: 143 us; the launch traced here: 142 us
  blocking collectives  56.1 us (39%)
  starting transfers between devices  42.4 us (30%)
  waiting for transfers between devices  27.5 us (19%)
  Pallas kernels  13.8 us (10%)
  local copies, waits for them, and re-layouts  1.68 us (1%)
    all_to_all x2, blocking collectives, local(): recv = lax.all_to_all(send, PLANE, split_axis=0, concat_axis=0, tiled=True)  56.1 us
    all_to_all x2, starting transfers between devices, exchange(): lax.all_to_all(rows, DP, split_axis=0, concat_axis=0, axis_index_groups=o...  27 us
    ppermute x6, waiting for transfers between devices, swap(): return lax.ppermute(part, QUAD, [(at, at ^ hop) for at in range(4)])  19.9 us
    ppermute x6, starting transfers between devices, swap(): return lax.ppermute(part, QUAD, [(at, at ^ hop) for at in range(4)])  15.4 us
    all_to_all x2, waiting for transfers between devices, exchange(): lax.all_to_all(rows, DP, split_axis=0, concat_axis=0, axis_index_groups=o...  7.64 us
  transfers between devices with their start and end apart: 8, of which 6 were waited for; matrix products, arithmetic and copies ran while one was open for 0% of the time, Pallas kernels for 4%

profile of v4, /device:TPU:1, one launch (start us, length us, event | category | flops | bytes accessed | tf_op | source)
XLA Modules:
  0.0 142.4 jit_solution(9991681728325862333)
XLA Ops:
  0.6 0.0 copy-start.1
  0.6 0.0 copy-start
  0.7 1.7 %share.1 = bf16[512,384]{1,0:T(8,128)(2,1)} custom-call(bf16[8,2,128]{2,1,0:T(2,128)(2,1)} %refs_0_.1, bf16[8,2,128]{2,1,0:T(2,128)(2,1)} %refs_1_.1, bf16[8,2,128]{2,1,0:T(2,128)(2,1)} %refs_2_.1, bf16[8,2,128]{2,1,0:T(2,128)(2,1)} %refs_3_.1, bf16[8,2,128]{2,1,0:T(2,128)(2,1)} %refs_4_.1, bf16[8,2,128]{2,1,0:T(2,128)(2,1)} %refs_5_.1), custom_call_target="tpu_custom_call" | custom-call | tf_op jit(solution)/shard_map/share/pallas_call | solution.py:317
  2.4 18.1 %all-to-all-start = ((bf16[64,8,384]{2,1,0:T(8,128)(2,1)}), bf16[64,8,384]{2,1,0:T(8,128)(2,1)S(1)}, u32[]{:S(2)}, u32[]{:S(2)}) async-start(bf16[64,8,384]{2,1,0:T(8,128)(2,1)} %bitcast.17), calls=%async_computation | async-start | bytes 786432 | tf_op jit(solution)/shard_map/all_to_all | solution.py:297
  20.5 2.1 %far.1 = (bf16[512,256]{1,0:T(8,128)(2,1)}, bf16[512,256]{1,0:T(8,128)(2,1)}) custom-call(s32[1]{0:T(128)} %bitcast.quad_ref, bf16[256,1024]{1,0:T(8,128)(2,1)} %tok_ref.3, bf16[256,1024]{1,0:T(8,128)(2,1)} %cot_ref.3), custom_call_target="tpu_custom_call" | custom-call | tf_op jit(solution)/shard_map/far/pallas_call | solution.py:326
  22.5 3.6 %collective-permute-start.2 = (bf16[512,256]{1,0:T(8,128)(2,1)}, bf16[512,256]{1,0:T(8,128)(2,1)S(1)}, u32[]{:S(2)}, u32[]{:S(2)}) collective-permute-start(bf16[512,256]{1,0:T(8,128)(2,1)} %get-tuple-element.35), channel_id=1, source_target_pairs={{0,264},{8,256},{256,8},{264,0},{1,265},{9,257},{257,9},{265,1},{2... | collective-permute-start | bytes 786440 | tf_op jit(solution)/shard_map/ppermute | solution.py:303
  26.2 2.0 %collective-permute-start.1 = (bf16[512,256]{1,0:T(8,128)(2,1)}, bf16[512,256]{1,0:T(8,128)(2,1)S(1)}, u32[]{:S(2)}, u32[]{:S(2)}) collective-permute-start(bf16[512,256]{1,0:T(8,128)(2,1)} %get-tuple-element.32.after_ref), channel_id=1, source_target_pairs={{0,256},{8,264},{256,0},{264,8},{1,257},{9,265},{257,1},{265,9},{2... | collective-permute-start | bytes 786440 | tf_op jit(solution)/shard_map/ppermute | solution.py:303
  28.2 0.0 copy-start.4
  28.2 1.0 copy-done.4
  29.1 0.4 near.1
  29.6 0.7 copy-done.2
  30.3 2.2 %collective-permute-start = (bf16[512,256]{1,0:T(8,128)(2,1)S(1)}, bf16[512,256]{1,0:T(8,128)(2,1)S(1)}, u32[]{:S(2)}, u32[]{:S(2)}) collective-permute-start(bf16[512,256]{1,0:T(8,128)(2,1)S(1)} %get-tuple-element.34), channel_id=1, source_target_pairs={{0,8},{8,0},{256,264},{264,256},{1,9},{9,1},{257,265},{265,257},{2... | collective-permute-start | bytes 786440 | tf_op jit(solution)/shard_map/ppermute | solution.py:303
  32.5 2.7 %collective-permute-done.2.refs_3_ = bf16[512,256]{1,0:T(8,128)(2,1)S(1)} collective-permute-done((bf16[512,256]{1,0:T(8,128)(2,1)}, bf16[512,256]{1,0:T(8,128)(2,1)S(1)}, u32[]{:S(2)}, u32[]{:S(2)}) %collective-permute-start.2) | collective-permute-done | bytes 262176 | tf_op jit(solution)/shard_map/ppermute | solution.py:303
  35.2 6.7 %collective-permute-done.1.refs_2_ = bf16[512,256]{1,0:T(8,128)(2,1)S(1)} collective-permute-done((bf16[512,256]{1,0:T(8,128)(2,1)}, bf16[512,256]{1,0:T(8,128)(2,1)S(1)}, u32[]{:S(2)}, u32[]{:S(2)}) %collective-permute-start.1) | collective-permute-done | bytes 262176 | tf_op jit(solution)/shard_map/ppermute | solution.py:303
  41.9 3.8 %all-to-all-done = bf16[64,8,384]{2,1,0:T(8,128)(2,1)S(1)} async-done(((bf16[64,8,384]{2,1,0:T(8,128)(2,1)}), bf16[64,8,384]{2,1,0:T(8,128)(2,1)S(1)}, u32[]{:S(2)}, u32[]{:S(2)}) %all-to-all-start) | async-done | bytes 393248 | tf_op jit(solution)/shard_map/all_to_all | solution.py:297
  45.6 1.3 first.1
  46.9 29.4 %all_to_all.44 = bf16[32,8,3072]{2,1,0:T(8,128)(2,1)S(1)} all-to-all(bf16[32,8,3072]{2,1,0:T(8,128)(2,1)S(1)} %bitcast.13), channel_id=1, replica_groups=mesh['xlo'=2,'z'=16,'core'=2,'xhi'=2,'y'=4] {'xhi','y','xlo','core'}, dimensions={0} | all-to-all | bytes 3145728 | tf_op jit(solution)/shard_map/all_to_all | solution.py:343
  76.3 2.2 %middle.1 = (bf16[256,3072]{1,0:T(8,128)(2,1)S(1)}, bf16[256,384]{1,0:T(8,128)(2,1)S(1)}) custom-call(bf16[256,768]{1,0:T(8,128)(2,1)S(1)} %get-tuple-element.37.weights_ref, bf16[256,3072]{1,0:T(8,128)(2,1)S(1)} %bitcast.12, bf16[256,256]{1,0:T(8,128)(2,1)S(1)} %get-tuple-element.39.pairs_ref.refs_6_, ...), custom_call_target="tpu_custom_call" | custom-call | tf_op jit(solution)/shard_map/middle/pallas_call | solution.py:344
  78.6 26.7 %all_to_all.45 = bf16[32,8,3072]{2,1,0:T(8,128)(2,1)S(1)} all-to-all(bf16[32,8,3072]{2,1,0:T(8,128)(2,1)S(1)} %bitcast.14), channel_id=1, replica_groups=mesh['xlo'=2,'z'=16,'core'=2,'xhi'=2,'y'=4] {'xhi','y','xlo','core'}, dimensions={0} | all-to-all | bytes 3145728 | tf_op jit(solution)/shard_map/all_to_all | solution.py:347
  105.3 2.2 %inner.1 = bf16[512,384]{1,0:T(8,128)(2,1)} custom-call(s32[1]{0:T(128)} %bitcast.quad_ref, bf16[512,256]{1,0:T(8,128)(2,1)S(1)} %get-tuple-element.33.refs_0_, bf16[512,256]{1,0:T(8,128)(2,1)S(1)} %collective-permute-done.refs_1_, bf16[512,256]{1,0:T(8,128)(2,1)S(1)} %collective-permute-done.1.refs_2_, bf16[512,256]{1,0:T(8,128)(2,1)S(1)} %collective-permute-done.2.refs_3_, ...), custom_call_target="tpu_custom_call" | custom-call | tf_op jit(solution)/shard_map/inner/pallas_call | solution.py:348
  107.5 8.9 %all-to-all-start.3 = ((bf16[64,8,384]{2,1,0:T(8,128)(2,1)}), bf16[64,8,384]{2,1,0:T(8,128)(2,1)S(1)}, u32[]{:S(2)}, u32[]{:S(2)}) async-start(bf16[64,8,384]{2,1,0:T(8,128)(2,1)} %bitcast.7), calls=%async_computation.3 | async-start | bytes 786432 | tf_op jit(solution)/shard_map/all_to_all | solution.py:297
  116.4 1.1 output.1
  117.4 3.6 %collective-permute-start.3 = (bf16[512,256]{1,0:T(8,128)(2,1)S(1)}, bf16[512,256]{1,0:T(8,128)(2,1)S(1)}, u32[]{:S(2)}, u32[]{:S(2)}) collective-permute-start(bf16[512,256]{1,0:T(8,128)(2,1)S(1)} %get-tuple-element.41), channel_id=1, source_target_pairs={{0,264},{8,256},{256,8},{264,0},{1,265},{9,257},{257,9},{265,1},{2... | collective-permute-start | bytes 786440 | tf_op jit(solution)/shard_map/ppermute | solution.py:303
  121.1 2.0 %collective-permute-start.5 = (bf16[512,256]{1,0:T(8,128)(2,1)S(1)}, bf16[512,256]{1,0:T(8,128)(2,1)S(1)}, u32[]{:S(2)}, u32[]{:S(2)}) collective-permute-start(bf16[512,256]{1,0:T(8,128)(2,1)S(1)} %get-tuple-element.44), channel_id=1, source_target_pairs={{0,256},{8,264},{256,0},{264,8},{1,257},{9,265},{257,1},{265,9},{2... | collective-permute-start | bytes 786440 | tf_op jit(solution)/shard_map/ppermute | solution.py:303
  123.1 6.9 %collective-permute-done.3.refs_0_.three_ref = bf16[512,256]{1,0:T(8,128)(2,1)S(1)} collective-permute-done((bf16[512,256]{1,0:T(8,128)(2,1)S(1)}, bf16[512,256]{1,0:T(8,128)(2,1)S(1)}, u32[]{:S(2)}, u32[]{:S(2)}) %collective-permute-start.3) | collective-permute-done | bytes 262176 | tf_op jit(solution)/shard_map/ppermute | solution.py:303
  130.0 1.0 output2.1
  131.1 1.9 %collective-permute-start.4 = (bf16[512,256]{1,0:T(8,128)(2,1)S(1)}, bf16[512,256]{1,0:T(8,128)(2,1)S(1)}, u32[]{:S(2)}, u32[]{:S(2)}) collective-permute-start(bf16[512,256]{1,0:T(8,128)(2,1)S(1)} %get-tuple-element.43), channel_id=1, source_target_pairs={{0,8},{8,0},{256,264},{264,256},{1,9},{9,1},{257,265},{265,257},{2... | collective-permute-start | bytes 786440 | tf_op jit(solution)/shard_map/ppermute | solution.py:303
  133.0 3.6 %collective-permute-done.5.two_ref = bf16[512,256]{1,0:T(8,128)(2,1)S(1)} collective-permute-done((bf16[512,256]{1,0:T(8,128)(2,1)S(1)}, bf16[512,256]{1,0:T(8,128)(2,1)S(1)}, u32[]{:S(2)}, u32[]{:S(2)}) %collective-permute-start.5) | collective-permute-done | bytes 262176 | tf_op jit(solution)/shard_map/ppermute | solution.py:303
  136.6 0.0 collective-permute-done.4.one_ref
  136.6 1.1 place.1
  137.7 3.9 %all-to-all-done.3 = bf16[64,8,384]{2,1,0:T(8,128)(2,1)S(1)} async-done(((bf16[64,8,384]{2,1,0:T(8,128)(2,1)}), bf16[64,8,384]{2,1,0:T(8,128)(2,1)S(1)}, u32[]{:S(2)}, u32[]{:S(2)}) %all-to-all-start.3) | async-done | bytes 393248 | tf_op jit(solution)/shard_map/all_to_all | solution.py:297
  141.6 0.8 end.1
  (6 shorter events, 0.0 us)
Async XLA Ops:
  0.6 27.5 %copy-start.1 = (bf16[256,1024]{1,0:T(8,128)(2,1)S(1)}, bf16[256,1024]{1,0:T(8,128)(2,1)}, u32[]{:S(2)}) copy-start(bf16[256,1024]{1,0:T(8,128)(2,1)} %cot_ref.3) | copy-start | bytes 1572868
  0.6 27.5 %copy-start = (bf16[256,1024]{1,0:T(8,128)(2,1)S(1)}, bf16[256,1024]{1,0:T(8,128)(2,1)}, u32[]{:S(2)}) copy-start(bf16[256,1024]{1,0:T(8,128)(2,1)} %tok_ref.3) | copy-start | bytes 1572868
  2.4 43.3 %all-to-all-start = ((bf16[64,8,384]{2,1,0:T(8,128)(2,1)}), bf16[64,8,384]{2,1,0:T(8,128)(2,1)S(1)}, u32[]{:S(2)}, u32[]{:S(2)}) async-start(bf16[64,8,384]{2,1,0:T(8,128)(2,1)} %bitcast.17), calls=%async_computation | async-start | bytes 786432 | tf_op jit(solution)/shard_map/all_to_all | solution.py:297
  22.5 12.7 %collective-permute-start.2 = (bf16[512,256]{1,0:T(8,128)(2,1)}, bf16[512,256]{1,0:T(8,128)(2,1)S(1)}, u32[]{:S(2)}, u32[]{:S(2)}) collective-permute-start(bf16[512,256]{1,0:T(8,128)(2,1)} %get-tuple-element.35), channel_id=1, source_target_pairs={{0,264},{8,256},{256,8},{264,0},{1,265},{9,257},{257,9},{265,1},{2... | collective-permute-start | bytes 786440 | tf_op jit(solution)/shard_map/ppermute | solution.py:303
  26.2 15.7 %collective-permute-start.1 = (bf16[512,256]{1,0:T(8,128)(2,1)}, bf16[512,256]{1,0:T(8,128)(2,1)S(1)}, u32[]{:S(2)}, u32[]{:S(2)}) collective-permute-start(bf16[512,256]{1,0:T(8,128)(2,1)} %get-tuple-element.32.after_ref), channel_id=1, source_target_pairs={{0,256},{8,264},{256,0},{264,8},{1,257},{9,265},{257,1},{265,9},{2... | collective-permute-start | bytes 786440 | tf_op jit(solution)/shard_map/ppermute | solution.py:303
  28.2 1.0 copy-start.4
  29.6 0.7 copy-start.2
  30.3 11.6 %collective-permute-start = (bf16[512,256]{1,0:T(8,128)(2,1)S(1)}, bf16[512,256]{1,0:T(8,128)(2,1)S(1)}, u32[]{:S(2)}, u32[]{:S(2)}) collective-permute-start(bf16[512,256]{1,0:T(8,128)(2,1)S(1)} %get-tuple-element.34), channel_id=1, source_target_pairs={{0,8},{8,0},{256,264},{264,256},{1,9},{9,1},{257,265},{265,257},{2... | collective-permute-start | bytes 786440 | tf_op jit(solution)/shard_map/ppermute | solution.py:303
  78.5 26.8 %copy-start.3 = (bf16[512,256]{1,0:T(8,128)(2,1)S(1)}, bf16[512,256]{1,0:T(8,128)(2,1)}, u32[]{:S(2)}) copy-start(bf16[512,256]{1,0:T(8,128)(2,1)} %copy-done.2) | copy-start | bytes 786436
  107.5 34.1 %all-to-all-start.3 = ((bf16[64,8,384]{2,1,0:T(8,128)(2,1)}), bf16[64,8,384]{2,1,0:T(8,128)(2,1)S(1)}, u32[]{:S(2)}, u32[]{:S(2)}) async-start(bf16[64,8,384]{2,1,0:T(8,128)(2,1)} %bitcast.7), calls=%async_computation.3 | async-start | bytes 786432 | tf_op jit(solution)/shard_map/all_to_all | solution.py:297
  117.4 12.6 %collective-permute-start.3 = (bf16[512,256]{1,0:T(8,128)(2,1)S(1)}, bf16[512,256]{1,0:T(8,128)(2,1)S(1)}, u32[]{:S(2)}, u32[]{:S(2)}) collective-permute-start(bf16[512,256]{1,0:T(8,128)(2,1)S(1)} %get-tuple-element.41), channel_id=1, source_target_pairs={{0,264},{8,256},{256,8},{264,0},{1,265},{9,257},{257,9},{265,1},{2... | collective-permute-start | bytes 786440 | tf_op jit(solution)/shard_map/ppermute | solution.py:303
  121.1 15.5 %collective-permute-start.5 = (bf16[512,256]{1,0:T(8,128)(2,1)S(1)}, bf16[512,256]{1,0:T(8,128)(2,1)S(1)}, u32[]{:S(2)}, u32[]{:S(2)}) collective-permute-start(bf16[512,256]{1,0:T(8,128)(2,1)S(1)} %get-tuple-element.44), channel_id=1, source_target_pairs={{0,256},{8,264},{256,0},{264,8},{1,257},{9,265},{257,1},{265,9},{2... | collective-permute-start | bytes 786440 | tf_op jit(solution)/shard_map/ppermute | solution.py:303
  131.1 5.5 %collective-permute-start.4 = (bf16[512,256]{1,0:T(8,128)(2,1)S(1)}, bf16[512,256]{1,0:T(8,128)(2,1)S(1)}, u32[]{:S(2)}, u32[]{:S(2)}) collective-permute-start(bf16[512,256]{1,0:T(8,128)(2,1)S(1)} %get-tuple-element.43), channel_id=1, source_target_pairs={{0,8},{8,0},{256,264},{264,256},{1,9},{9,1},{257,265},{265,257},{2... | collective-permute-start | bytes 786440 | tf_op jit(solution)/shard_map/ppermute | solution.py:303

commit v5 on v4

--- a/solution.py
+++ b/solution.py
@@ -130,9 +130,22 @@
     ref[TOK:, :] = cot_ref[:, cols]
 
 
-def far_kernel(quad_ref, tok_ref, cot_ref, two_ref, three_ref):
-    cut_piece(quad_ref, tok_ref, cot_ref, 2, two_ref)
-    cut_piece(quad_ref, tok_ref, cot_ref, 3, three_ref)
+def far_kernel(quad_ref, tok_ref, cot_ref, two_ref, three_ref, sems):
+    copies = []
+    for at, ref in enumerate((two_ref, three_ref)):
+        cols = pl.ds(pl.multiple_of((quad_ref[0] ^ (2 + at)) * PAIR, PAIR), PAIR)
+        for which, source in enumerate((tok_ref, cot_ref)):
+            copies.append(
+                pltpu.make_async_copy(
+                    source.at[:, cols],
+                    ref.at[which * TOK : (which + 1) * TOK, :],
+                    sems.at[2 * at + which],
+                )
+            )
+    for copy in copies:
+        copy.start()
+    for copy in copies:
+        copy.wait()
 
 
 def near_kernel(quad_ref, tok_ref, cot_ref, after_ref, own_ref, one_ref, *order_refs):
@@ -156,12 +169,16 @@
     gate = dot(quads, dot(nat, factor_of(weights, 0), 1, 0).astype(BF), 1, 1).astype(BF)
     value = dot(quads, dot(nat, factor_of(weights, 1), 1, 0).astype(BF), 1, 1).astype(BF)
     down = factor_of(weights, 2)
-    for hop, ref in enumerate(piece_refs):
+    tok = jnp.concatenate([ref[:TOK, :] for ref in piece_refs], axis=0)
+    cot = jnp.concatenate([ref[TOK:, :] for ref in piece_refs], axis=0)
+    first = dot(jnp.concatenate([gate, value], axis=0), tok, 1, 1).astype(BF)
+    back = dot(down, cot, 1, 1).astype(BF)
+    for hop in range(4):
         at = pl.multiple_of((quad_ref[0] ^ hop) * TOK, TOK)
-        tok, cot = ref[:TOK, :], ref[TOK:, :]
-        send_ref[:, pl.ds(at, TOK)] = dot(gate, tok, 1, 1).astype(BF)
-        send_ref[:, pl.ds(SLAB + at, TOK)] = dot(value, tok, 1, 1).astype(BF)
-        send_ref[:, pl.ds(2 * SLAB + at, TOK)] = dot(down, cot, 1, 1).astype(BF)
+        cols = slice(hop * TOK, (hop + 1) * TOK)
+        send_ref[:, pl.ds(at, TOK)] = first[:PAIR, cols]
+        send_ref[:, pl.ds(SLAB + at, TOK)] = first[PAIR:, cols]
+        send_ref[:, pl.ds(2 * SLAB + at, TOK)] = back[:, cols]
 
 
 def middle_kernel(
@@ -213,15 +230,17 @@
         refs[4:],
     )
     pairs, quads = pairs_ref[...], quads_ref[...]
-    gate_grad = value_grad = down_grad = 0.0
-    for hop, ref in enumerate(piece_refs):
-        at = pl.multiple_of((quad_ref[0] ^ hop) * TOK, TOK)
-        tok, cot = ref[:TOK, :], ref[TOK:, :]
-        gate_grad += dot(recv_ref[:, pl.ds(SLAB + at, TOK)], tok, 1, 0)
-        value_grad += dot(recv_ref[:, pl.ds(2 * SLAB + at, TOK)], tok, 1, 0)
-        down_grad += dot(recv_ref[:, pl.ds(at, TOK)], cot, 1, 0)
-    gate_grad = dot(pairs, gate_grad.astype(BF), 1, 1).astype(BF)
-    value_grad = dot(pairs, value_grad.astype(BF), 1, 1).astype(BF)
+    tok = jnp.concatenate([ref[:TOK, :] for ref in piece_refs], axis=0)
+    cot = jnp.concatenate([ref[TOK:, :] for ref in piece_refs], axis=0)
+
+    def columns(first):
+        at = [first + pl.multiple_of((quad_ref[0] ^ hop) * TOK, TOK) for hop in range(4)]
+        return jnp.concatenate([recv_ref[:, pl.ds(start, TOK)] for start in at], axis=1)
+
+    both = dot(jnp.concatenate([columns(SLAB), columns(2 * SLAB)], axis=0), tok, 1, 0)
+    down_grad = dot(columns(0), cot, 1, 0)
+    both = dot(pairs, both.astype(BF), 1, 1).astype(BF)
+    gate_grad, value_grad = both[:, :PAIR], both[:, PAIR:]
     inner = jnp.concatenate(
         [
             own_block(dot(gate_grad, quads, 1, 0)).astype(BF),
@@ -323,11 +342,17 @@
         in_specs=[pl.BlockSpec(memory_space=pl.ANY)] * 6,
     )(gate_inner, value_inner, down_outer, gate_outer, value_outer, down_inner)
     shares = exchange(shares)
-    two, three = call(far_kernel, "far", (piece,) * 2, room=60, in_specs=scalar_first(2))(
-        quad, tokens, cotangent
-    )
+    anywhere = pl.BlockSpec(memory_space=pl.ANY)
+    two, three = call(
+        far_kernel,
+        "far",
+        (piece,) * 2,
+        [pltpu.SemaphoreType.DMA((4,))],
+        room=60,
+        in_specs=scalar_first(0) + [anywhere] * 2,
+    )(quad, tokens, cotangent)
     square, tall = shape((PAIR, PAIR)), shape((2 * PAIR, PAIR))
-    after = [pl.BlockSpec(memory_space=pl.ANY)]
+    after = [anywhere]
     own, one, pairs, quads, *owners = call(
         near_kernel,
         "near",

time: 143 us -> 143 us (level)
  no operation moved by 1% of the time
where the time goes in v5:
time: 143 us; the launch traced here: 142 us
  blocking collectives  56.1 us (39%)
  starting transfers between devices  42.3 us (30%)
  waiting for transfers between devices  27.6 us (19%)
  Pallas kernels  13.7 us (10%)
  local copies, waits for them, and re-layouts  1.68 us (1%)
    all_to_all x2, blocking collectives, local(): recv = lax.all_to_all(send, PLANE, split_axis=0, concat_axis=0, tiled=True)  56.1 us
    all_to_all x2, starting transfers between devices, exchange(): lax.all_to_all(rows, DP, split_axis=0, concat_axis=0, axis_index_groups=o...  26.9 us
    ppermute x6, waiting for transfers between devices, swap(): return lax.ppermute(part, QUAD, [(at, at ^ hop) for at in range(4)])  20 us
    ppermute x6, starting transfers between devices, swap(): return lax.ppermute(part, QUAD, [(at, at ^ hop) for at in range(4)])  15.4 us
    all_to_all x2, waiting for transfers between devices, exchange(): lax.all_to_all(rows, DP, split_axis=0, concat_axis=0, axis_index_groups=o...  7.69 us
  transfers between devices with their start and end apart: 8, of which 6 were waited for; matrix products, arithmetic and copies ran while one was open for 0% of the time, Pallas kernels for 4%

profile of v5, /device:TPU:1, one launch (start us, length us, event | category | flops | bytes accessed | tf_op | source)
XLA Modules:
  0.0 142.3 jit_solution(6140183060529734370)
XLA Ops:
  0.6 0.0 copy-start.1
  0.6 0.0 copy-start
  0.7 1.7 %share.1 = bf16[512,384]{1,0:T(8,128)(2,1)} custom-call(bf16[8,2,128]{2,1,0:T(2,128)(2,1)} %refs_0_.1, bf16[8,2,128]{2,1,0:T(2,128)(2,1)} %refs_1_.1, bf16[8,2,128]{2,1,0:T(2,128)(2,1)} %refs_2_.1, bf16[8,2,128]{2,1,0:T(2,128)(2,1)} %refs_3_.1, bf16[8,2,128]{2,1,0:T(2,128)(2,1)} %refs_4_.1, bf16[8,2,128]{2,1,0:T(2,128)(2,1)} %refs_5_.1), custom_call_target="tpu_custom_call" | custom-call | tf_op jit(solution)/shard_map/share/pallas_call | solution.py:336
  2.4 18.1 %all-to-all-start = ((bf16[64,8,384]{2,1,0:T(8,128)(2,1)}), bf16[64,8,384]{2,1,0:T(8,128)(2,1)S(1)}, u32[]{:S(2)}, u32[]{:S(2)}) async-start(bf16[64,8,384]{2,1,0:T(8,128)(2,1)} %bitcast.17), calls=%async_computation | async-start | bytes 786432 | tf_op jit(solution)/shard_map/all_to_all | solution.py:316
  20.5 1.9 %far.1 = (bf16[512,256]{1,0:T(8,128)(2,1)}, bf16[512,256]{1,0:T(8,128)(2,1)}) custom-call(s32[1]{0:T(128)} %bitcast.quad_ref, bf16[256,1024]{1,0:T(8,128)(2,1)} %tok_ref.3, bf16[256,1024]{1,0:T(8,128)(2,1)} %cot_ref.3), custom_call_target="tpu_custom_call" | custom-call | tf_op jit(solution)/shard_map/far/pallas_call | solution.py:346
  22.4 3.6 %collective-permute-start.2 = (bf16[512,256]{1,0:T(8,128)(2,1)}, bf16[512,256]{1,0:T(8,128)(2,1)S(1)}, u32[]{:S(2)}, u32[]{:S(2)}) collective-permute-start(bf16[512,256]{1,0:T(8,128)(2,1)} %get-tuple-element.35), channel_id=1, source_target_pairs={{0,264},{8,256},{256,8},{264,0},{1,265},{9,257},{257,9},{265,1},{2... | collective-permute-start | bytes 786440 | tf_op jit(solution)/shard_map/ppermute | solution.py:322
  26.0 2.0 %collective-permute-start.1 = (bf16[512,256]{1,0:T(8,128)(2,1)}, bf16[512,256]{1,0:T(8,128)(2,1)S(1)}, u32[]{:S(2)}, u32[]{:S(2)}) collective-permute-start(bf16[512,256]{1,0:T(8,128)(2,1)} %get-tuple-element.32.after_ref), channel_id=1, source_target_pairs={{0,256},{8,264},{256,0},{264,8},{1,257},{9,265},{257,1},{265,9},{2... | collective-permute-start | bytes 786440 | tf_op jit(solution)/shard_map/ppermute | solution.py:322
  28.0 0.0 copy-start.4
  28.1 1.0 copy-done.4
  29.0 0.4 near.1
  29.4 0.7 copy-done.2
  30.1 2.2 %collective-permute-start = (bf16[512,256]{1,0:T(8,128)(2,1)S(1)}, bf16[512,256]{1,0:T(8,128)(2,1)S(1)}, u32[]{:S(2)}, u32[]{:S(2)}) collective-permute-start(bf16[512,256]{1,0:T(8,128)(2,1)S(1)} %get-tuple-element.34), channel_id=1, source_target_pairs={{0,8},{8,0},{256,264},{264,256},{1,9},{9,1},{257,265},{265,257},{2... | collective-permute-start | bytes 786440 | tf_op jit(solution)/shard_map/ppermute | solution.py:322
  32.4 2.7 %collective-permute-done.2.refs_3_ = bf16[512,256]{1,0:T(8,128)(2,1)S(1)} collective-permute-done((bf16[512,256]{1,0:T(8,128)(2,1)}, bf16[512,256]{1,0:T(8,128)(2,1)S(1)}, u32[]{:S(2)}, u32[]{:S(2)}) %collective-permute-start.2) | collective-permute-done | bytes 262176 | tf_op jit(solution)/shard_map/ppermute | solution.py:322
  35.1 6.7 %collective-permute-done.1.refs_2_ = bf16[512,256]{1,0:T(8,128)(2,1)S(1)} collective-permute-done((bf16[512,256]{1,0:T(8,128)(2,1)}, bf16[512,256]{1,0:T(8,128)(2,1)S(1)}, u32[]{:S(2)}, u32[]{:S(2)}) %collective-permute-start.1) | collective-permute-done | bytes 262176 | tf_op jit(solution)/shard_map/ppermute | solution.py:322
  41.8 0.0 collective-permute-done.refs_1_
  41.8 3.8 %all-to-all-done = bf16[64,8,384]{2,1,0:T(8,128)(2,1)S(1)} async-done(((bf16[64,8,384]{2,1,0:T(8,128)(2,1)}), bf16[64,8,384]{2,1,0:T(8,128)(2,1)S(1)}, u32[]{:S(2)}, u32[]{:S(2)}) %all-to-all-start) | async-done | bytes 393248 | tf_op jit(solution)/shard_map/all_to_all | solution.py:316
  45.6 1.3 first.1
  46.9 29.4 %all_to_all.44 = bf16[32,8,3072]{2,1,0:T(8,128)(2,1)S(1)} all-to-all(bf16[32,8,3072]{2,1,0:T(8,128)(2,1)S(1)} %bitcast.13), channel_id=1, replica_groups=mesh['xlo'=2,'z'=16,'core'=2,'xhi'=2,'y'=4] {'xhi','y','xlo','core'}, dimensions={0} | all-to-all | bytes 3145728 | tf_op jit(solution)/shard_map/all_to_all | solution.py:368
  76.3 2.2 %middle.1 = (bf16[256,3072]{1,0:T(8,128)(2,1)S(1)}, bf16[256,384]{1,0:T(8,128)(2,1)S(1)}) custom-call(bf16[256,768]{1,0:T(8,128)(2,1)S(1)} %get-tuple-element.37.weights_ref, bf16[256,3072]{1,0:T(8,128)(2,1)S(1)} %bitcast.12, bf16[256,256]{1,0:T(8,128)(2,1)S(1)} %get-tuple-element.39.pairs_ref.refs_6_, ...), custom_call_target="tpu_custom_call" | custom-call | tf_op jit(solution)/shard_map/middle/pallas_call | solution.py:369
  78.5 26.7 %all_to_all.45 = bf16[32,8,3072]{2,1,0:T(8,128)(2,1)S(1)} all-to-all(bf16[32,8,3072]{2,1,0:T(8,128)(2,1)S(1)} %bitcast.14), channel_id=1, replica_groups=mesh['xlo'=2,'z'=16,'core'=2,'xhi'=2,'y'=4] {'xhi','y','xlo','core'}, dimensions={0} | all-to-all | bytes 3145728 | tf_op jit(solution)/shard_map/all_to_all | solution.py:372
  105.3 2.2 %inner.1 = bf16[512,384]{1,0:T(8,128)(2,1)} custom-call(s32[1]{0:T(128)} %bitcast.quad_ref, bf16[512,256]{1,0:T(8,128)(2,1)S(1)} %get-tuple-element.33.refs_0_, bf16[512,256]{1,0:T(8,128)(2,1)S(1)} %collective-permute-done.refs_1_, bf16[512,256]{1,0:T(8,128)(2,1)S(1)} %collective-permute-done.1.refs_2_, bf16[512,256]{1,0:T(8,128)(2,1)S(1)} %collective-permute-done.2.refs_3_, ...), custom_call_target="tpu_custom_call" | custom-call | tf_op jit(solution)/shard_map/inner/pallas_call | solution.py:373
  107.5 8.8 %all-to-all-start.3 = ((bf16[64,8,384]{2,1,0:T(8,128)(2,1)}), bf16[64,8,384]{2,1,0:T(8,128)(2,1)S(1)}, u32[]{:S(2)}, u32[]{:S(2)}) async-start(bf16[64,8,384]{2,1,0:T(8,128)(2,1)} %bitcast.7), calls=%async_computation.3 | async-start | bytes 786432 | tf_op jit(solution)/shard_map/all_to_all | solution.py:316
  116.3 1.1 output.1
  117.4 3.6 %collective-permute-start.3 = (bf16[512,256]{1,0:T(8,128)(2,1)S(1)}, bf16[512,256]{1,0:T(8,128)(2,1)S(1)}, u32[]{:S(2)}, u32[]{:S(2)}) collective-permute-start(bf16[512,256]{1,0:T(8,128)(2,1)S(1)} %get-tuple-element.41), channel_id=1, source_target_pairs={{0,264},{8,256},{256,8},{264,0},{1,265},{9,257},{257,9},{265,1},{2... | collective-permute-start | bytes 786440 | tf_op jit(solution)/shard_map/ppermute | solution.py:322
  121.0 2.0 %collective-permute-start.5 = (bf16[512,256]{1,0:T(8,128)(2,1)S(1)}, bf16[512,256]{1,0:T(8,128)(2,1)S(1)}, u32[]{:S(2)}, u32[]{:S(2)}) collective-permute-start(bf16[512,256]{1,0:T(8,128)(2,1)S(1)} %get-tuple-element.44), channel_id=1, source_target_pairs={{0,256},{8,264},{256,0},{264,8},{1,257},{9,265},{257,1},{265,9},{2... | collective-permute-start | bytes 786440 | tf_op jit(solution)/shard_map/ppermute | solution.py:322
  123.0 6.9 %collective-permute-done.3.refs_0_.three_ref = bf16[512,256]{1,0:T(8,128)(2,1)S(1)} collective-permute-done((bf16[512,256]{1,0:T(8,128)(2,1)S(1)}, bf16[512,256]{1,0:T(8,128)(2,1)S(1)}, u32[]{:S(2)}, u32[]{:S(2)}) %collective-permute-start.3) | collective-permute-done | bytes 262176 | tf_op jit(solution)/shard_map/ppermute | solution.py:322
  129.9 1.0 output2.1
  131.0 1.9 %collective-permute-start.4 = (bf16[512,256]{1,0:T(8,128)(2,1)S(1)}, bf16[512,256]{1,0:T(8,128)(2,1)S(1)}, u32[]{:S(2)}, u32[]{:S(2)}) collective-permute-start(bf16[512,256]{1,0:T(8,128)(2,1)S(1)} %get-tuple-element.43), channel_id=1, source_target_pairs={{0,8},{8,0},{256,264},{264,256},{1,9},{9,1},{257,265},{265,257},{2... | collective-permute-start | bytes 786440 | tf_op jit(solution)/shard_map/ppermute | solution.py:322
  132.9 3.6 %collective-permute-done.5.two_ref = bf16[512,256]{1,0:T(8,128)(2,1)S(1)} collective-permute-done((bf16[512,256]{1,0:T(8,128)(2,1)S(1)}, bf16[512,256]{1,0:T(8,128)(2,1)S(1)}, u32[]{:S(2)}, u32[]{:S(2)}) %collective-permute-start.5) | collective-permute-done | bytes 262176 | tf_op jit(solution)/shard_map/ppermute | solution.py:322
  136.5 1.1 place.1
  137.6 3.9 %all-to-all-done.3 = bf16[64,8,384]{2,1,0:T(8,128)(2,1)S(1)} async-done(((bf16[64,8,384]{2,1,0:T(8,128)(2,1)}), bf16[64,8,384]{2,1,0:T(8,128)(2,1)S(1)}, u32[]{:S(2)}, u32[]{:S(2)}) %all-to-all-start.3) | async-done | bytes 393248 | tf_op jit(solution)/shard_map/all_to_all | solution.py:316
  141.5 0.8 end.1
  (6 shorter events, 0.0 us)
Async XLA Ops:
  0.6 27.4 %copy-start.1 = (bf16[256,1024]{1,0:T(8,128)(2,1)S(1)}, bf16[256,1024]{1,0:T(8,128)(2,1)}, u32[]{:S(2)}) copy-start(bf16[256,1024]{1,0:T(8,128)(2,1)} %cot_ref.3) | copy-start | bytes 1572868
  0.6 27.4 %copy-start = (bf16[256,1024]{1,0:T(8,128)(2,1)S(1)}, bf16[256,1024]{1,0:T(8,128)(2,1)}, u32[]{:S(2)}) copy-start(bf16[256,1024]{1,0:T(8,128)(2,1)} %tok_ref.3) | copy-start | bytes 1572868
  2.4 43.3 %all-to-all-start = ((bf16[64,8,384]{2,1,0:T(8,128)(2,1)}), bf16[64,8,384]{2,1,0:T(8,128)(2,1)S(1)}, u32[]{:S(2)}, u32[]{:S(2)}) async-start(bf16[64,8,384]{2,1,0:T(8,128)(2,1)} %bitcast.17), calls=%async_computation | async-start | bytes 786432 | tf_op jit(solution)/shard_map/all_to_all | solution.py:316
  22.4 12.7 %collective-permute-start.2 = (bf16[512,256]{1,0:T(8,128)(2,1)}, bf16[512,256]{1,0:T(8,128)(2,1)S(1)}, u32[]{:S(2)}, u32[]{:S(2)}) collective-permute-start(bf16[512,256]{1,0:T(8,128)(2,1)} %get-tuple-element.35), channel_id=1, source_target_pairs={{0,264},{8,256},{256,8},{264,0},{1,265},{9,257},{257,9},{265,1},{2... | collective-permute-start | bytes 786440 | tf_op jit(solution)/shard_map/ppermute | solution.py:322
  26.0 15.8 %collective-permute-start.1 = (bf16[512,256]{1,0:T(8,128)(2,1)}, bf16[512,256]{1,0:T(8,128)(2,1)S(1)}, u32[]{:S(2)}, u32[]{:S(2)}) collective-permute-start(bf16[512,256]{1,0:T(8,128)(2,1)} %get-tuple-element.32.after_ref), channel_id=1, source_target_pairs={{0,256},{8,264},{256,0},{264,8},{1,257},{9,265},{257,1},{265,9},{2... | collective-permute-start | bytes 786440 | tf_op jit(solution)/shard_map/ppermute | solution.py:322
  28.0 1.0 copy-start.4
  29.4 0.7 copy-start.2
  30.1 11.7 %collective-permute-start = (bf16[512,256]{1,0:T(8,128)(2,1)S(1)}, bf16[512,256]{1,0:T(8,128)(2,1)S(1)}, u32[]{:S(2)}, u32[]{:S(2)}) collective-permute-start(bf16[512,256]{1,0:T(8,128)(2,1)S(1)} %get-tuple-element.34), channel_id=1, source_target_pairs={{0,8},{8,0},{256,264},{264,256},{1,9},{9,1},{257,265},{265,257},{2... | collective-permute-start | bytes 786440 | tf_op jit(solution)/shard_map/ppermute | solution.py:322
  78.5 26.8 %copy-start.3 = (bf16[512,256]{1,0:T(8,128)(2,1)S(1)}, bf16[512,256]{1,0:T(8,128)(2,1)}, u32[]{:S(2)}) copy-start(bf16[512,256]{1,0:T(8,128)(2,1)} %copy-done.2) | copy-start | bytes 786436
  107.5 34.0 %all-to-all-start.3 = ((bf16[64,8,384]{2,1,0:T(8,128)(2,1)}), bf16[64,8,384]{2,1,0:T(8,128)(2,1)S(1)}, u32[]{:S(2)}, u32[]{:S(2)}) async-start(bf16[64,8,384]{2,1,0:T(8,128)(2,1)} %bitcast.7), calls=%async_computation.3 | async-start | bytes 786432 | tf_op jit(solution)/shard_map/all_to_all | solution.py:316
  117.4 12.6 %collective-permute-start.3 = (bf16[512,256]{1,0:T(8,128)(2,1)S(1)}, bf16[512,256]{1,0:T(8,128)(2,1)S(1)}, u32[]{:S(2)}, u32[]{:S(2)}) collective-permute-start(bf16[512,256]{1,0:T(8,128)(2,1)S(1)} %get-tuple-element.41), channel_id=1, source_target_pairs={{0,264},{8,256},{256,8},{264,0},{1,265},{9,257},{257,9},{265,1},{2... | collective-permute-start | bytes 786440 | tf_op jit(solution)/shard_map/ppermute | solution.py:322
  121.0 15.5 %collective-permute-start.5 = (bf16[512,256]{1,0:T(8,128)(2,1)S(1)}, bf16[512,256]{1,0:T(8,128)(2,1)S(1)}, u32[]{:S(2)}, u32[]{:S(2)}) collective-permute-start(bf16[512,256]{1,0:T(8,128)(2,1)S(1)} %get-tuple-element.44), channel_id=1, source_target_pairs={{0,256},{8,264},{256,0},{264,8},{1,257},{9,265},{257,1},{265,9},{2... | collective-permute-start | bytes 786440 | tf_op jit(solution)/shard_map/ppermute | solution.py:322
  131.0 5.5 %collective-permute-start.4 = (bf16[512,256]{1,0:T(8,128)(2,1)S(1)}, bf16[512,256]{1,0:T(8,128)(2,1)S(1)}, u32[]{:S(2)}, u32[]{:S(2)}) collective-permute-start(bf16[512,256]{1,0:T(8,128)(2,1)S(1)} %get-tuple-element.43), channel_id=1, source_target_pairs={{0,8},{8,0},{256,264},{264,256},{1,9},{9,1},{257,265},{265,257},{2... | collective-permute-start | bytes 786440 | tf_op jit(solution)/shard_map/ppermute | solution.py:322

commit v6 on v5

--- a/solution.py
+++ b/solution.py
@@ -54,11 +54,11 @@
 
 
 def device_at(place):
-    return place >> 5, (((place >> 1) & 15) * STEP) & 15, place & 1
+    return place & 1, (((place >> 1) & 15) * STEP) & 15, place >> 5
 
 
 def place_of(device):
-    return (device >> 5) * 32 + (((device >> 1) & 15) * STEP & 15) * 2 + (device & 1)
+    return (device & 1) * 32 + (((device >> 1) & 15) * STEP & 15) * 2 + (device >> 5)
 
 
 def device_index(place):

time: 143 us -> 143 us (level); the launches traced: 142 us -> 140 us
  waiting for transfers between devices: 27.6 us -> 23.5 us
  blocking collectives: 56.1 us -> 57.7 us
    all_to_all x2, waiting for transfers between devices: 7.69 us -> 4.76 us  [exchange(): lax.all_to_all(rows, DP, split_axis=0, concat_axis=0, axis_index_groups=o...]
    all_to_all x2, blocking collectives: 56.1 us -> 57.7 us  [local(): recv = lax.all_to_all(send, PLANE, split_axis=0, concat_axis=0, tiled=True)]
where the time goes in v6:
time: 143 us; the launch traced here: 140 us
  blocking collectives  57.7 us (40%)
  starting transfers between devices  43.1 us (30%)
  waiting for transfers between devices  23.5 us (16%)
  Pallas kernels  13.7 us (10%)
  local copies, waits for them, and re-layouts  1.68 us (1%)
    all_to_all x2, blocking collectives, local(): recv = lax.all_to_all(send, PLANE, split_axis=0, concat_axis=0, tiled=True)  57.7 us
    all_to_all x2, starting transfers between devices, exchange(): lax.all_to_all(rows, DP, split_axis=0, concat_axis=0, axis_index_groups=o...  27.8 us
    ppermute x6, waiting for transfers between devices, swap(): return lax.ppermute(part, QUAD, [(at, at ^ hop) for at in range(4)])  18.7 us
    ppermute x6, starting transfers between devices, swap(): return lax.ppermute(part, QUAD, [(at, at ^ hop) for at in range(4)])  15.3 us
    all_to_all x2, waiting for transfers between devices, exchange(): lax.all_to_all(rows, DP, split_axis=0, concat_axis=0, axis_index_groups=o...  4.76 us
  transfers between devices with their start and end apart: 8, of which 6 were waited for; matrix products, arithmetic and copies ran while one was open for 0% of the time, Pallas kernels for 4%

profile of v6, /device:TPU:1, one launch (start us, length us, event | category | flops | bytes accessed | tf_op | source)
XLA Modules:
  0.0 140.4 jit_solution(3545021832808599767)
XLA Ops:
  0.6 0.0 copy-start.1
  0.6 0.0 copy-start
  0.7 1.7 %share.1 = bf16[512,384]{1,0:T(8,128)(2,1)} custom-call(bf16[8,2,128]{2,1,0:T(2,128)(2,1)} %refs_0_.1, bf16[8,2,128]{2,1,0:T(2,128)(2,1)} %refs_1_.1, bf16[8,2,128]{2,1,0:T(2,128)(2,1)} %refs_2_.1, bf16[8,2,128]{2,1,0:T(2,128)(2,1)} %refs_3_.1, bf16[8,2,128]{2,1,0:T(2,128)(2,1)} %refs_4_.1, bf16[8,2,128]{2,1,0:T(2,128)(2,1)} %refs_5_.1), custom_call_target="tpu_custom_call" | custom-call | tf_op jit(solution)/shard_map/share/pallas_call | solution.py:336
  2.4 18.2 %all-to-all-start = ((bf16[64,8,384]{2,1,0:T(8,128)(2,1)}), bf16[64,8,384]{2,1,0:T(8,128)(2,1)S(1)}, u32[]{:S(2)}, u32[]{:S(2)}) async-start(bf16[64,8,384]{2,1,0:T(8,128)(2,1)} %bitcast.17), calls=%async_computation | async-start | bytes 786432 | tf_op jit(solution)/shard_map/all_to_all | solution.py:316
  20.6 1.9 %far.1 = (bf16[512,256]{1,0:T(8,128)(2,1)}, bf16[512,256]{1,0:T(8,128)(2,1)}) custom-call(s32[1]{0:T(128)} %bitcast.quad_ref, bf16[256,1024]{1,0:T(8,128)(2,1)} %tok_ref.3, bf16[256,1024]{1,0:T(8,128)(2,1)} %cot_ref.3), custom_call_target="tpu_custom_call" | custom-call | tf_op jit(solution)/shard_map/far/pallas_call | solution.py:346
  22.5 3.4 %collective-permute-start.2 = (bf16[512,256]{1,0:T(8,128)(2,1)}, bf16[512,256]{1,0:T(8,128)(2,1)S(1)}, u32[]{:S(2)}, u32[]{:S(2)}) collective-permute-start(bf16[512,256]{1,0:T(8,128)(2,1)} %get-tuple-element.35), channel_id=1, source_target_pairs={{0,264},{8,256},{256,8},{264,0},{1,265},{9,257},{257,9},{265,1},{2... | collective-permute-start | bytes 786440 | tf_op jit(solution)/shard_map/ppermute | solution.py:322
  25.9 2.1 %collective-permute-start.1 = (bf16[512,256]{1,0:T(8,128)(2,1)}, bf16[512,256]{1,0:T(8,128)(2,1)S(1)}, u32[]{:S(2)}, u32[]{:S(2)}) collective-permute-start(bf16[512,256]{1,0:T(8,128)(2,1)} %get-tuple-element.32.after_ref), channel_id=1, source_target_pairs={{0,256},{8,264},{256,0},{264,8},{1,257},{9,265},{257,1},{265,9},{2... | collective-permute-start | bytes 786440 | tf_op jit(solution)/shard_map/ppermute | solution.py:322
  28.0 0.0 copy-start.4
  28.1 1.0 copy-done.4
  29.0 0.4 near.1
  29.4 0.7 copy-done.2
  30.1 2.3 %collective-permute-start = (bf16[512,256]{1,0:T(8,128)(2,1)S(1)}, bf16[512,256]{1,0:T(8,128)(2,1)S(1)}, u32[]{:S(2)}, u32[]{:S(2)}) collective-permute-start(bf16[512,256]{1,0:T(8,128)(2,1)S(1)} %get-tuple-element.34), channel_id=1, source_target_pairs={{0,8},{8,0},{256,264},{264,256},{1,9},{9,1},{257,265},{265,257},{2... | collective-permute-start | bytes 786440 | tf_op jit(solution)/shard_map/ppermute | solution.py:322
  32.5 2.9 %collective-permute-done.2.refs_3_ = bf16[512,256]{1,0:T(8,128)(2,1)S(1)} collective-permute-done((bf16[512,256]{1,0:T(8,128)(2,1)}, bf16[512,256]{1,0:T(8,128)(2,1)S(1)}, u32[]{:S(2)}, u32[]{:S(2)}) %collective-permute-start.2) | collective-permute-done | bytes 262176 | tf_op jit(solution)/shard_map/ppermute | solution.py:322
  35.4 5.7 %collective-permute-done.1.refs_2_ = bf16[512,256]{1,0:T(8,128)(2,1)S(1)} collective-permute-done((bf16[512,256]{1,0:T(8,128)(2,1)}, bf16[512,256]{1,0:T(8,128)(2,1)S(1)}, u32[]{:S(2)}, u32[]{:S(2)}) %collective-permute-start.1) | collective-permute-done | bytes 262176 | tf_op jit(solution)/shard_map/ppermute | solution.py:322
  41.1 0.0 collective-permute-done.refs_1_
  41.1 2.5 %all-to-all-done = bf16[64,8,384]{2,1,0:T(8,128)(2,1)S(1)} async-done(((bf16[64,8,384]{2,1,0:T(8,128)(2,1)}), bf16[64,8,384]{2,1,0:T(8,128)(2,1)S(1)}, u32[]{:S(2)}, u32[]{:S(2)}) %all-to-all-start) | async-done | bytes 393248 | tf_op jit(solution)/shard_map/all_to_all | solution.py:316
  43.6 1.3 first.1
  44.9 30.9 %all_to_all.44 = bf16[32,8,3072]{2,1,0:T(8,128)(2,1)S(1)} all-to-all(bf16[32,8,3072]{2,1,0:T(8,128)(2,1)S(1)} %bitcast.13), channel_id=1, replica_groups=mesh['xlo'=2,'z'=16,'core'=2,'xhi'=2,'y'=4] {'xhi','y','xlo','core'}, dimensions={0} | all-to-all | bytes 3145728 | tf_op jit(solution)/shard_map/all_to_all | solution.py:368
  75.8 2.2 %middle.1 = (bf16[256,3072]{1,0:T(8,128)(2,1)S(1)}, bf16[256,384]{1,0:T(8,128)(2,1)S(1)}) custom-call(bf16[256,768]{1,0:T(8,128)(2,1)S(1)} %get-tuple-element.37.weights_ref, bf16[256,3072]{1,0:T(8,128)(2,1)S(1)} %bitcast.12, bf16[256,256]{1,0:T(8,128)(2,1)S(1)} %get-tuple-element.39.pairs_ref.refs_6_, ...), custom_call_target="tpu_custom_call" | custom-call | tf_op jit(solution)/shard_map/middle/pallas_call | solution.py:369
  78.0 26.8 %all_to_all.45 = bf16[32,8,3072]{2,1,0:T(8,128)(2,1)S(1)} all-to-all(bf16[32,8,3072]{2,1,0:T(8,128)(2,1)S(1)} %bitcast.14), channel_id=1, replica_groups=mesh['xlo'=2,'z'=16,'core'=2,'xhi'=2,'y'=4] {'xhi','y','xlo','core'}, dimensions={0} | all-to-all | bytes 3145728 | tf_op jit(solution)/shard_map/all_to_all | solution.py:372
  104.8 2.2 %inner.1 = bf16[512,384]{1,0:T(8,128)(2,1)} custom-call(s32[1]{0:T(128)} %bitcast.quad_ref, bf16[512,256]{1,0:T(8,128)(2,1)S(1)} %get-tuple-element.33.refs_0_, bf16[512,256]{1,0:T(8,128)(2,1)S(1)} %collective-permute-done.refs_1_, bf16[512,256]{1,0:T(8,128)(2,1)S(1)} %collective-permute-done.1.refs_2_, bf16[512,256]{1,0:T(8,128)(2,1)S(1)} %collective-permute-done.2.refs_3_, ...), custom_call_target="tpu_custom_call" | custom-call | tf_op jit(solution)/shard_map/inner/pallas_call | solution.py:373
  106.9 9.6 %all-to-all-start.3 = ((bf16[64,8,384]{2,1,0:T(8,128)(2,1)}), bf16[64,8,384]{2,1,0:T(8,128)(2,1)S(1)}, u32[]{:S(2)}, u32[]{:S(2)}) async-start(bf16[64,8,384]{2,1,0:T(8,128)(2,1)} %bitcast.7), calls=%async_computation.3 | async-start | bytes 786432 | tf_op jit(solution)/shard_map/all_to_all | solution.py:316
  116.5 1.1 output.1
  117.6 3.4 %collective-permute-start.3 = (bf16[512,256]{1,0:T(8,128)(2,1)S(1)}, bf16[512,256]{1,0:T(8,128)(2,1)S(1)}, u32[]{:S(2)}, u32[]{:S(2)}) collective-permute-start(bf16[512,256]{1,0:T(8,128)(2,1)S(1)} %get-tuple-element.41), channel_id=1, source_target_pairs={{0,264},{8,256},{256,8},{264,0},{1,265},{9,257},{257,9},{265,1},{2... | collective-permute-start | bytes 786440 | tf_op jit(solution)/shard_map/ppermute | solution.py:322
  121.1 2.1 %collective-permute-start.5 = (bf16[512,256]{1,0:T(8,128)(2,1)S(1)}, bf16[512,256]{1,0:T(8,128)(2,1)S(1)}, u32[]{:S(2)}, u32[]{:S(2)}) collective-permute-start(bf16[512,256]{1,0:T(8,128)(2,1)S(1)} %get-tuple-element.44), channel_id=1, source_target_pairs={{0,256},{8,264},{256,0},{264,8},{1,257},{9,265},{257,1},{265,9},{2... | collective-permute-start | bytes 786440 | tf_op jit(solution)/shard_map/ppermute | solution.py:322
  123.2 6.8 %collective-permute-done.3.refs_0_.three_ref = bf16[512,256]{1,0:T(8,128)(2,1)S(1)} collective-permute-done((bf16[512,256]{1,0:T(8,128)(2,1)S(1)}, bf16[512,256]{1,0:T(8,128)(2,1)S(1)}, u32[]{:S(2)}, u32[]{:S(2)}) %collective-permute-start.3) | collective-permute-done | bytes 262176 | tf_op jit(solution)/shard_map/ppermute | solution.py:322
  130.0 1.0 output2.1
  131.0 1.9 %collective-permute-start.4 = (bf16[512,256]{1,0:T(8,128)(2,1)S(1)}, bf16[512,256]{1,0:T(8,128)(2,1)S(1)}, u32[]{:S(2)}, u32[]{:S(2)}) collective-permute-start(bf16[512,256]{1,0:T(8,128)(2,1)S(1)} %get-tuple-element.43), channel_id=1, source_target_pairs={{0,8},{8,0},{256,264},{264,256},{1,9},{9,1},{257,265},{265,257},{2... | collective-permute-start | bytes 786440 | tf_op jit(solution)/shard_map/ppermute | solution.py:322
  133.0 3.3 %collective-permute-done.5.two_ref = bf16[512,256]{1,0:T(8,128)(2,1)S(1)} collective-permute-done((bf16[512,256]{1,0:T(8,128)(2,1)S(1)}, bf16[512,256]{1,0:T(8,128)(2,1)S(1)}, u32[]{:S(2)}, u32[]{:S(2)}) %collective-permute-start.5) | collective-permute-done | bytes 262176 | tf_op jit(solution)/shard_map/ppermute | solution.py:322
  136.2 1.1 place.1
  137.3 2.3 %all-to-all-done.3 = bf16[64,8,384]{2,1,0:T(8,128)(2,1)S(1)} async-done(((bf16[64,8,384]{2,1,0:T(8,128)(2,1)}), bf16[64,8,384]{2,1,0:T(8,128)(2,1)S(1)}, u32[]{:S(2)}, u32[]{:S(2)}) %all-to-all-start.3) | async-done | bytes 393248 | tf_op jit(solution)/shard_map/all_to_all | solution.py:316
  139.6 0.8 end.1
  (6 shorter events, 0.0 us)
Async XLA Ops:
  0.6 27.4 %copy-start.1 = (bf16[256,1024]{1,0:T(8,128)(2,1)S(1)}, bf16[256,1024]{1,0:T(8,128)(2,1)}, u32[]{:S(2)}) copy-start(bf16[256,1024]{1,0:T(8,128)(2,1)} %cot_ref.3) | copy-start | bytes 1572868
  0.6 27.4 %copy-start = (bf16[256,1024]{1,0:T(8,128)(2,1)S(1)}, bf16[256,1024]{1,0:T(8,128)(2,1)}, u32[]{:S(2)}) copy-start(bf16[256,1024]{1,0:T(8,128)(2,1)} %tok_ref.3) | copy-start | bytes 1572868
  2.4 41.3 %all-to-all-start = ((bf16[64,8,384]{2,1,0:T(8,128)(2,1)}), bf16[64,8,384]{2,1,0:T(8,128)(2,1)S(1)}, u32[]{:S(2)}, u32[]{:S(2)}) async-start(bf16[64,8,384]{2,1,0:T(8,128)(2,1)} %bitcast.17), calls=%async_computation | async-start | bytes 786432 | tf_op jit(solution)/shard_map/all_to_all | solution.py:316
  22.5 12.9 %collective-permute-start.2 = (bf16[512,256]{1,0:T(8,128)(2,1)}, bf16[512,256]{1,0:T(8,128)(2,1)S(1)}, u32[]{:S(2)}, u32[]{:S(2)}) collective-permute-start(bf16[512,256]{1,0:T(8,128)(2,1)} %get-tuple-element.35), channel_id=1, source_target_pairs={{0,264},{8,256},{256,8},{264,0},{1,265},{9,257},{257,9},{265,1},{2... | collective-permute-start | bytes 786440 | tf_op jit(solution)/shard_map/ppermute | solution.py:322
  25.9 15.2 %collective-permute-start.1 = (bf16[512,256]{1,0:T(8,128)(2,1)}, bf16[512,256]{1,0:T(8,128)(2,1)S(1)}, u32[]{:S(2)}, u32[]{:S(2)}) collective-permute-start(bf16[512,256]{1,0:T(8,128)(2,1)} %get-tuple-element.32.after_ref), channel_id=1, source_target_pairs={{0,256},{8,264},{256,0},{264,8},{1,257},{9,265},{257,1},{265,9},{2... | collective-permute-start | bytes 786440 | tf_op jit(solution)/shard_map/ppermute | solution.py:322
  28.0 1.0 copy-start.4
  29.4 0.7 copy-start.2
  30.1 11.0 %collective-permute-start = (bf16[512,256]{1,0:T(8,128)(2,1)S(1)}, bf16[512,256]{1,0:T(8,128)(2,1)S(1)}, u32[]{:S(2)}, u32[]{:S(2)}) collective-permute-start(bf16[512,256]{1,0:T(8,128)(2,1)S(1)} %get-tuple-element.34), channel_id=1, source_target_pairs={{0,8},{8,0},{256,264},{264,256},{1,9},{9,1},{257,265},{265,257},{2... | collective-permute-start | bytes 786440 | tf_op jit(solution)/shard_map/ppermute | solution.py:322
  78.0 26.8 %copy-start.3 = (bf16[512,256]{1,0:T(8,128)(2,1)S(1)}, bf16[512,256]{1,0:T(8,128)(2,1)}, u32[]{:S(2)}) copy-start(bf16[512,256]{1,0:T(8,128)(2,1)} %copy-done.2) | copy-start | bytes 786436
  106.9 32.7 %all-to-all-start.3 = ((bf16[64,8,384]{2,1,0:T(8,128)(2,1)}), bf16[64,8,384]{2,1,0:T(8,128)(2,1)S(1)}, u32[]{:S(2)}, u32[]{:S(2)}) async-start(bf16[64,8,384]{2,1,0:T(8,128)(2,1)} %bitcast.7), calls=%async_computation.3 | async-start | bytes 786432 | tf_op jit(solution)/shard_map/all_to_all | solution.py:316
  117.6 12.4 %collective-permute-start.3 = (bf16[512,256]{1,0:T(8,128)(2,1)S(1)}, bf16[512,256]{1,0:T(8,128)(2,1)S(1)}, u32[]{:S(2)}, u32[]{:S(2)}) collective-permute-start(bf16[512,256]{1,0:T(8,128)(2,1)S(1)} %get-tuple-element.41), channel_id=1, source_target_pairs={{0,264},{8,256},{256,8},{264,0},{1,265},{9,257},{257,9},{265,1},{2... | collective-permute-start | bytes 786440 | tf_op jit(solution)/shard_map/ppermute | solution.py:322
  121.1 15.2 %collective-permute-start.5 = (bf16[512,256]{1,0:T(8,128)(2,1)S(1)}, bf16[512,256]{1,0:T(8,128)(2,1)S(1)}, u32[]{:S(2)}, u32[]{:S(2)}) collective-permute-start(bf16[512,256]{1,0:T(8,128)(2,1)S(1)} %get-tuple-element.44), channel_id=1, source_target_pairs={{0,256},{8,264},{256,0},{264,8},{1,257},{9,265},{257,1},{265,9},{2... | collective-permute-start | bytes 786440 | tf_op jit(solution)/shard_map/ppermute | solution.py:322
  131.0 5.2 %collective-permute-start.4 = (bf16[512,256]{1,0:T(8,128)(2,1)S(1)}, bf16[512,256]{1,0:T(8,128)(2,1)S(1)}, u32[]{:S(2)}, u32[]{:S(2)}) collective-permute-start(bf16[512,256]{1,0:T(8,128)(2,1)S(1)} %get-tuple-element.43), channel_id=1, source_target_pairs={{0,8},{8,0},{256,264},{264,256},{1,9},{9,1},{257,265},{265,257},{2... | collective-permute-start | bytes 786440 | tf_op jit(solution)/shard_map/ppermute | solution.py:322
